TPU v7x, 512 devices: a whole 4x8x8 slice. The times are simulated.
512 devices in a mesh: dom: 128 (over z, y, core), field: 4 (over x).
Axes of the slice: x: 4, y: 8, z: 8, core: 2. Of those that a mesh axis runs over, the one named last changes fastest.
Arguments:
- traces: float32 [8, 28, 65536], P('field', None, 'dom'), may hold values from -6 to 6
- interior_source: bfloat16 [8, 84, 32768], P('field', None, 'dom'), may hold values from -6 to 6
- orders: int32 [32768], P('dom'), may hold values from 2 to 6, as said below
- element_scale: float32 [32768], P('dom'), may hold values from 0.5 to 2
- element_faces: int32 [4, 32768], P(None, 'dom'), may hold values from 0 to 65535, as said below
- solver_slots: int32 [65536], P('dom'), may hold values from 0 to 511, as said below
- line_diagonal: float32 [8, 65536], P('field', 'dom'), may hold values from 2.5 to 6
- species_mix: float32 [8, 8], P('field'), may hold values from -3 to 3
- couple_in: bfloat16 [672, 896], P('field'), may hold values from -0.1875 to 0.1875
- local_inverse: bfloat16 [672, 672], P('field'), may hold values from -0.25 to 0.25
- trace_block: bfloat16 [896, 896], P('field'), may hold values from -0.1875 to 0.1875
- couple_out: bfloat16 [896, 672], P('field'), may hold values from -0.25 to 0.25
Outputs:
- new_traces: float32 [8, 28, 65536], P('field', None, 'dom')
- mixed: float32 [8, 28, 65536], P('field', None, 'dom')
Inputs may be any that keep to these rules, and one draw needn't show every extreme that they name: `element_faces`: each face is named by exactly two (element, face) entries. The elements of partition d name the faces owned by d, the last 32 faces of partition d - 1 and the first 32 faces of partition d + 1, with partitions counted cyclically. `orders`: orders are higher on some partitions than on others. `solver_slots`: each partition's 512 entries are a permutation of 0 to 511.
All inputs are finite; a program needn't handle non-finite values.
Results may differ from a plain program's by a relative error of at most 0.0029.
The roundings to bfloat16 on the way count: a program that leaves them out, or rounds other values in their place, can miss the bound.
Values may be sent and summed in bfloat16 or wider, within the bound.
A program may use at most 64 MiB of HBM per device.

v0:
```python
import jax
import jax.numpy as jnp
from jax import lax
from jax.sharding import PartitionSpec as P

NFD = 28
NID = 84
DEG = 3


cheb_center = 1.0
cheb_half = 0.8
cheb_ratio = 1.25


def extended_2(shard, sides, width, wrap):
    for axis, dim in sides:
        devices, length = (lax.axis_size(axis), shard.shape[dim])
        up = [(i, (i + 1) % devices) for i in range(devices if wrap else devices - 1)]
        down = [(j, i) for i, j in up]
        last = lax.slice_in_dim(shard, length - width, length, axis=dim)
        leading = lax.slice_in_dim(shard, 0, width, axis=dim)
        before = lax.ppermute(last, axis, up)
        after = lax.ppermute(leading, axis, down)
        shard = jnp.concatenate([before, shard, after], axis=dim)
    return shard


def passed_along(block, axis, distance):
    devices = range(lax.axis_size(axis))
    route = [((i - distance) % len(devices), i) for i in devices]
    return lax.ppermute(block, axis, route)


def live_masks(orders, comps):
    face_count = (orders + 1) * (orders + 2) // 2
    inner_count = (orders + 1) * (orders + 2) * (orders + 3) // 6
    face_one = jnp.arange(NFD, dtype=jnp.int32)[:, None] < face_count[None, :]
    face_live = jnp.tile(face_one, (4, 1))
    inner_one = jnp.arange(NID, dtype=jnp.int32)[:, None] < inner_count[None, :]
    return (face_live, jnp.tile(face_live, (comps, 1)), jnp.tile(inner_one, (comps, 1)))


def cheb_sweep(resid, inverse, apply_line):
    step_vec = inverse * resid / cheb_center
    total = step_vec
    rho = 1.0 / cheb_ratio
    for sweep_index in range(DEG - 1):
        rho_next = 1.0 / (2.0 * cheb_ratio - rho)
        step_vec = rho_next * rho * step_vec + 2.0 * rho_next / cheb_half * inverse * (
            resid - apply_line(total)
        )
        total = total + step_vec
        rho = rho_next
    return total


def two_sweeps(resid, inverse, apply_line):
    first = cheb_sweep(resid, inverse, apply_line)
    second = cheb_sweep(resid - apply_line(first), inverse, apply_line)
    return first + second


def shards(
    traces,
    interior_source,
    orders,
    element_scale,
    element_faces,
    solver_slots,
    line_diagonal,
    species_mix,
    couple_in,
    local_inverse,
    trace_block,
    couple_out,
):
    comps = traces.shape[0]
    faces = traces.shape[2]
    elements = orders.shape[0]
    part_index = lax.axis_index("dom")
    total_faces = lax.axis_size("dom") * faces
    extended = extended_2(traces.astype(jnp.bfloat16), (("dom", 2),), faces, True).astype(
        traces.dtype
    )
    relative = (element_faces - part_index * faces) % total_faces
    local_ids = jnp.where(relative >= total_faces - faces, relative - total_faces, relative) + faces
    flat_ids = local_ids.reshape(-1)
    face_one, face_own, inner_own = live_masks(orders, comps)
    picked = extended[:, :, flat_ids].reshape(comps, NFD, 4, elements)
    picked = jnp.transpose(picked, (0, 2, 1, 3)).reshape(comps, 4 * NFD, elements)
    gathered_own = jnp.where(face_one[None], picked, 0.0).astype(jnp.bfloat16)
    gathered_all = lax.all_gather(gathered_own, "field", axis=0, tiled=True).reshape(-1, elements)
    source_own = interior_source.reshape(comps * NID, elements).astype(jnp.float32)
    loads_own = source_own - jnp.dot(couple_in, gathered_all, preferred_element_type=jnp.float32)
    loads_own = jnp.where(inner_own, loads_own, 0.0).astype(jnp.bfloat16)
    loads_all = lax.all_gather(loads_own, "field", axis=0, tiled=True)
    interior_own = jnp.dot(local_inverse, loads_all, preferred_element_type=jnp.float32)
    interior_own = jnp.where(inner_own, interior_own, 0.0).astype(jnp.bfloat16)
    interior_all = lax.all_gather(interior_own, "field", axis=0, tiled=True)
    blocks = jnp.dot(trace_block, gathered_all, preferred_element_type=jnp.float32) + jnp.dot(
        couple_out, interior_all, preferred_element_type=jnp.float32
    )
    blocks = jnp.where(face_own, blocks, 0.0) * element_scale[None, :]
    spread = (
        blocks.reshape(comps, 4, NFD, elements)
        .transpose(0, 2, 1, 3)
        .reshape(comps, NFD, 4 * elements)
    )
    summed = jnp.zeros((comps, NFD, faces + 2 * faces), jnp.float32).at[:, :, flat_ids].add(spread)
    owned = summed[:, :, faces : faces + faces]
    left_part = summed[:, :, :faces]
    right_part = summed[:, :, faces + faces :]
    from_next = passed_along(left_part.astype(jnp.bfloat16), "dom", -1).astype(left_part.dtype)
    from_prev = passed_along(right_part.astype(jnp.bfloat16), "dom", 1).astype(right_part.dtype)
    residual = owned.at[:, :, faces - faces :].add(from_next).at[:, :, :faces].add(from_prev)
    every_comp = lax.all_gather(residual, "field", axis=0, tiled=True)
    mixed = residual + jnp.einsum(
        "cd,dkf->ckf", species_mix, every_comp, precision=lax.Precision.HIGHEST
    )
    sendable = mixed[:, :, solver_slots]
    line_rhs = lax.all_to_all(sendable, "dom", split_axis=2, concat_axis=2, tiled=True)
    line_diag = line_diagonal[:, None, :]
    inverse = 1.0 / line_diag

    def apply_line(values):
        widened = extended_2(values, (("dom", 2),), 1, False)
        return line_diag * values - (widened[:, :, :-2] + widened[:, :, 2:])

    correction = two_sweeps(line_rhs, inverse, apply_line)
    returned = lax.all_to_all(correction, "dom", split_axis=2, concat_axis=2, tiled=True)
    owner_order = jnp.zeros_like(returned).at[:, :, solver_slots].set(returned)
    return (traces - owner_order, mixed)


def solution(mesh):
    in_specs = (
        P("field", None, "dom"),
        P("field", None, "dom"),
        P("dom"),
        P("dom"),
        P(None, "dom"),
        P("dom"),
        P("field", "dom"),
        P("field", None),
        P("field", None),
        P("field", None),
        P("field", None),
        P("field", None),
    )
    out_specs = (P("field", None, "dom"), P("field", None, "dom"))
    return jax.shard_map(shards, mesh=mesh, in_specs=in_specs, out_specs=out_specs, check_vma=False)
```

profile of v0, /device:TPU:1, one launch (start us, length us, event | category | flops | bytes accessed | tf_op | source)
XLA Modules:
  0.0 252.1 jit_solution(5131542040993880195)
XLA Ops:
  1.6 4.6 %collective-permute-start = (bf16[2,28,512]{2,0,1:T(2,128)(2,1)S(1)}, bf16[2,28,512]{2,0,1:T(2,128)(2,1)S(1)}, u32[]{:S(2)}, u32[]{:S(2)}) collective-permute-start(bf16[2,28,512]{2,0,1:T(2,128)(2,1)S(1)} %convert_element_type.29), channel_id=1, source_target_pairs={{0,4},{4,8},{8,12},{12,16},{16,20},{20,24},{24,28},{28,32},{32,36}... | collective-permute-start | bytes 172040 | tf_op jit(solution)/shard_map/ppermute | solution.py:23
  6.2 6.1 %collective-permute-start.1 = (bf16[2,28,512]{2,0,1:T(2,128)(2,1)S(1)}, bf16[2,28,512]{2,0,1:T(2,128)(2,1)S(1)}, u32[]{:S(2)}, u32[]{:S(2)}) collective-permute-start(bf16[2,28,512]{2,0,1:T(2,128)(2,1)S(1)} %convert_element_type.29), channel_id=1, source_target_pairs={{4,0},{8,4},{12,8},{16,12},{20,16},{24,20},{28,24},{32,28},{36,32}... | collective-permute-start | bytes 172040 | tf_op jit(solution)/shard_map/ppermute | solution.py:24
  16.5 3.7 %gather_fusion = bf16[1024,2,28]{2,1,0:T(2,128)(2,1)S(1)} fusion(bf16[2,28,1536]{1,0,2:T(2,128)(2,1)S(1)} %copy.118, s32[1024]{0:T(1024)S(1)} %broadcast_clamp_fusion), kind=kCustom, calls=%fused_computation | custom fusion | bytes 233472 | tf_op jit(solution)/shard_map/gather | solution.py:90
  20.8 9.8 %all_gather.12 = bf16[8,112,256]{2,1,0:T(8,128)(2,1)S(1)} all-gather(bf16[2,112,256]{2,1,0:T(8,128)(2,1)S(1)} %copy.120), channel_id=1, replica_groups=mesh['dom'=128,'field'=4] {'field'}, dimensions={0}, use_global_device_ids=true | all-gather | bytes 573440 | tf_op jit(solution)/shard_map/all_gather | solution.py:93
  30.8 9.7 %all_gather.13 = bf16[672,256]{1,0:T(8,128)(2,1)S(1)} all-gather(bf16[168,256]{1,0:T(8,128)(2,1)S(1)} %fusion.6), channel_id=1, replica_groups=mesh['dom'=128,'field'=4] {'field'}, dimensions={0}, use_global_device_ids=true | all-gather | bytes 430080 | tf_op jit(solution)/shard_map/all_gather | solution.py:97
  40.7 10.7 %all_gather.14 = bf16[672,256]{1,0:T(8,128)(2,1)S(1)} all-gather(bf16[168,256]{1,0:T(8,128)(2,1)S(1)} %fusion.7), channel_id=1, replica_groups=mesh['dom'=128,'field'=4] {'field'}, dimensions={0}, use_global_device_ids=true | all-gather | bytes 430080 | tf_op jit(solution)/shard_map/all_gather | solution.py:100
  53.4 32.8 %scatter_fusion = f32[2,28,1536]{1,0,2:T(2,128)S(1)} fusion(f32[2,28,1536]{1,0,2:T(2,128)S(1)} %broadcast_in_dim.39, s32[1024]{0:T(1024)S(1)} %bitcast.78, f32[1024,2,28]{2,1,0:T(2,128)S(1)} %copy.123), kind=kCustom, calls=%fused_computation.2 | custom fusion | flops 57344 | bytes 692224 | tf_op jit(solution)/shard_map/scatter-add | solution.py:110
  87.2 16.2 %collective-permute-start.2 = (bf16[2,28,512]{2,0,1:T(2,128)(2,1)S(1)}, bf16[2,28,512]{2,0,1:T(2,128)(2,1)S(1)}, u32[]{:S(2)}, u32[]{:S(2)}) collective-permute-start(bf16[2,28,512]{2,0,1:T(2,128)(2,1)S(1)} %get-tuple-element.68), channel_id=1, source_target_pairs={{4,0},{8,4},{12,8},{16,12},{20,16},{24,20},{28,24},{32,28},{36,32}... | collective-permute-start | bytes 172040 | tf_op jit(solution)/shard_map/ppermute | solution.py:32
  106.7 10.2 %all_gather.15 = f32[8,28,512]{2,1,0:T(8,128)S(1)} all-gather(f32[2,28,512]{2,1,0:T(8,128)S(1)} %copy.126), channel_id=1, replica_groups=mesh['dom'=128,'field'=4] {'field'}, dimensions={0}, use_global_device_ids=true | all-gather | bytes 573440 | tf_op jit(solution)/shard_map/all_gather | solution.py:117
  121.7 14.8 %all-to-all-start = ((f32[128,1,224]{2,1,0:T(1,128)}), f32[128,1,224]{2,1,0:T(1,128)S(1)}, u32[]{:S(2)}, u32[]{:S(2)}) async-start(f32[128,1,224]{2,1,0:T(1,128)} %reshape.221), calls=%async_computation | async-start | bytes 262144 | tf_op jit(solution)/shard_map/all_to_all | solution.py:122
  136.6 12.5 %all-to-all-done = f32[128,1,224]{2,1,0:T(1,128)S(1)} async-done(((f32[128,1,224]{2,1,0:T(1,128)}), f32[128,1,224]{2,1,0:T(1,128)S(1)}, u32[]{:S(2)}, u32[]{:S(2)}) %all-to-all-start) | async-done | bytes 114720 | tf_op jit(solution)/shard_map/all_to_all | solution.py:122
  152.1 2.7 %collective-permute-start.4 = (f32[2,28,1]{1,0,2:T(2,128)S(1)}, f32[2,28,1]{1,0,2:T(2,128)S(1)}, u32[]{:S(2)}, u32[]{:S(2)}) collective-permute-start(f32[2,28,1]{1,0,2:T(2,128)S(1)} %get-tuple-element.66), channel_id=1, source_target_pairs={{0,4},{4,8},{8,12},{12,16},{16,20},{20,24},{24,28},{28,32},{32,36}... | collective-permute-start | bytes 680 | tf_op jit(solution)/shard_map/ppermute | solution.py:23
  157.1 2.6 %collective-permute-done.5 = f32[2,28,1]{1,0,2:T(2,128)S(1)} collective-permute-done((f32[2,28,1]{1,0,2:T(2,128)S(1)}, f32[2,28,1]{1,0,2:T(2,128)S(1)}, u32[]{:S(2)}, u32[]{:S(2)}) %collective-permute-start.5) | collective-permute-done | bytes 256 | tf_op jit(solution)/shard_map/ppermute | solution.py:24
  163.5 2.5 %collective-permute-start.7 = (f32[2,28,1]{1,0,2:T(2,128)S(1)}, f32[2,28,1]{1,0,2:T(2,128)S(1)}, u32[]{:S(2)}, u32[]{:S(2)}) collective-permute-start(f32[2,28,1]{1,0,2:T(2,128)S(1)} %get-tuple-element.65), channel_id=1, source_target_pairs={{4,0},{8,4},{12,8},{16,12},{20,16},{24,20},{28,24},{32,28},{36,32}... | collective-permute-start | bytes 680 | tf_op jit(solution)/shard_map/ppermute | solution.py:24
  168.4 2.8 %add_add_fusion.1 = f32[2,28,512]{1,0,2:T(2,128)S(1)} fusion(f32[2,28,512]{1,0,2:T(2,128)S(1)} %fusion.32, f32[2,28,1]{1,0,2:T(2,128)S(1)} %collective-permute-done.7, f32[2,28,1]{1,0,2:T(2,128)S(1)} %collective-permute-done.6, f32[2,512]{0,1:T(8,128)S(1)} %copy.131, f32[2,512]{0,1:T(8,128)S(1)} %copy.130, f32[2,28,1]{1,0,2:T(2,128)S(1)} %collective-permute-done.5, ...), kind=kLoop, calls=%fused_computation.44 | loop fusion | flops 544768 | bytes 471936 | tf_op jit(solution)/shard_map/add | solution.py:53
  173.2 2.4 collective-permute-start.9
  175.6 2.5 collective-permute-done.9
  184.2 2.5 collective-permute-done.11
  190.5 2.5 collective-permute-start.13
  193.0 2.5 collective-permute-done.13
  195.5 2.9 %fusion.40 = f32[512,2,28]{2,1,0:T(2,128)S(1)} fusion(f32[2,28,512]{1,0,2:T(2,128)S(1)} %add_add_fusion.1, f32[2,28,512]{1,0,2:T(2,128)S(1)} %fusion.31, f32[2,28,512]{1,0,2:T(2,128)S(1)} %get-tuple-element.55, f32[2,28,1]{1,0,2:T(2,128)S(1)} %collective-permute-done.13, f32[2,28,1]{1,0,2:T(2,128)S(1)} %collective-permute-done.12, f32[2,512]{0,1:T(8,128)S(1)} %copy.131, ...), kind=kLoop, calls=%fused_computation.87 | loop fusion | flops 573440 | bytes 586624
  200.0 22.7 %all-to-all-start.1 = ((f32[128,1,224]{2,1,0:T(1,128)}), f32[128,1,224]{2,1,0:T(1,128)S(1)}, u32[]{:S(2)}, u32[]{:S(2)}) async-start(f32[128,1,224]{2,1,0:T(1,128)} %reshape.223), calls=%async_computation.1 | async-start | bytes 262144 | tf_op jit(solution)/shard_map/all_to_all | solution.py:131
  223.0 12.5 %all-to-all-done.1 = f32[128,1,224]{2,1,0:T(1,128)S(1)} async-done(((f32[128,1,224]{2,1,0:T(1,128)}), f32[128,1,224]{2,1,0:T(1,128)S(1)}, u32[]{:S(2)}, u32[]{:S(2)}) %all-to-all-start.1) | async-done | bytes 114720 | tf_op jit(solution)/shard_map/all_to_all | solution.py:131
  237.4 13.6 %scatter_fusion.1 = f32[2,28,512]{1,0,2:T(2,128)S(1)} fusion(f32[2,28,512]{1,0,2:T(2,128)S(1)} %broadcast_in_dim.37, s32[512]{0:T(512)S(1)} %compare_select_fusion.2, f32[512,2,28]{2,1,0:T(2,128)S(1)} %bitcast_bitcast_fusion), kind=kCustom, calls=%fused_computation.3 | custom fusion | bytes 346112 | tf_op jit(solution)/shard_map/scatter | solution.py:132
  (102 shorter events, 44.9 us)
Async XLA Ops:
  0.6 50.8 %copy-start = (bf16[224,896]{1,0:T(8,128)(2,1)S(1)}, bf16[224,896]{1,0:T(8,128)(2,1)}, u32[]{:S(2)}) copy-start(bf16[224,896]{1,0:T(8,128)(2,1)} %param.30) | copy-start | bytes 1204228
  1.6 13.9 %collective-permute-start = (bf16[2,28,512]{2,0,1:T(2,128)(2,1)S(1)}, bf16[2,28,512]{2,0,1:T(2,128)(2,1)S(1)}, u32[]{:S(2)}, u32[]{:S(2)}) collective-permute-start(bf16[2,28,512]{2,0,1:T(2,128)(2,1)S(1)} %convert_element_type.29), channel_id=1, source_target_pairs={{0,4},{4,8},{8,12},{12,16},{16,20},{20,24},{24,28},{28,32},{32,36}... | collective-permute-start | bytes 172040 | tf_op jit(solution)/shard_map/ppermute | solution.py:23
  6.2 9.3 %collective-permute-start.1 = (bf16[2,28,512]{2,0,1:T(2,128)(2,1)S(1)}, bf16[2,28,512]{2,0,1:T(2,128)(2,1)S(1)}, u32[]{:S(2)}, u32[]{:S(2)}) collective-permute-start(bf16[2,28,512]{2,0,1:T(2,128)(2,1)S(1)} %convert_element_type.29), channel_id=1, source_target_pairs={{4,0},{8,4},{12,8},{16,12},{20,16},{24,20},{28,24},{32,28},{36,32}... | collective-permute-start | bytes 172040 | tf_op jit(solution)/shard_map/ppermute | solution.py:24
  20.2 20.4 %copy-start.8 = (bf16[168,672]{1,0:T(8,128)(2,1)S(1)}, bf16[168,672]{1,0:T(8,128)(2,1)}, u32[]{:S(2)}) copy-start(bf16[168,672]{1,0:T(8,128)(2,1)} %param.29) | copy-start | bytes 677380
  30.8 20.9 %copy-start.3 = (bf16[224,672]{1,0:T(8,128)(2,1)S(1)}, bf16[224,672]{1,0:T(8,128)(2,1)}, u32[]{:S(2)}) copy-start(bf16[224,672]{1,0:T(8,128)(2,1)} %param.31) | copy-start | bytes 903172
  30.8 20.9 %copy-start.7 = (f32[256]{0:T(256)S(1)}, f32[256]{0:T(256)}, u32[]{:S(2)}) copy-start(f32[256]{0:T(256)} %param.23) | copy-start | bytes 3076
  86.2 30.7 %copy-start.6 = (f32[2,8]{1,0:T(2,128)S(1)}, f32[2,8]{1,0:T(2,128)}, u32[]{:S(2)}) copy-start(f32[2,8]{1,0:T(2,128)} %param.27) | copy-start | bytes 196
  87.2 18.2 %collective-permute-start.2 = (bf16[2,28,512]{2,0,1:T(2,128)(2,1)S(1)}, bf16[2,28,512]{2,0,1:T(2,128)(2,1)S(1)}, u32[]{:S(2)}, u32[]{:S(2)}) collective-permute-start(bf16[2,28,512]{2,0,1:T(2,128)(2,1)S(1)} %get-tuple-element.68), channel_id=1, source_target_pairs={{4,0},{8,4},{12,8},{16,12},{20,16},{24,20},{28,24},{32,28},{36,32}... | collective-permute-start | bytes 172040 | tf_op jit(solution)/shard_map/ppermute | solution.py:32
  103.4 3.2 %collective-permute-start.3 = (bf16[2,28,512]{2,0,1:T(2,128)(2,1)S(1)}, bf16[2,28,512]{2,0,1:T(2,128)(2,1)S(1)}, u32[]{:S(2)}, u32[]{:S(2)}) collective-permute-start(bf16[2,28,512]{2,0,1:T(2,128)(2,1)S(1)} %get-tuple-element.69), channel_id=1, source_target_pairs={{508,0},{0,4},{4,8},{8,12},{12,16},{16,20},{20,24},{24,28},{28,32}... | collective-permute-start | bytes 172040 | tf_op jit(solution)/shard_map/ppermute | solution.py:32
  117.7 18.9 %copy-start.2 = (f32[2,28,512]{2,0,1:T(2,128)}, f32[2,28,512]{2,0,1:T(2,128)S(1)}, u32[]{:S(2)}) copy-start(f32[2,28,512]{2,0,1:T(2,128)S(1)} %fusion.8) | copy-start | bytes 344068
  117.7 18.7 %copy-start.5 = (f32[2,512]{1,0:T(2,128)S(1)}, f32[2,512]{1,0:T(2,128)}, u32[]{:S(2)}) copy-start(f32[2,512]{1,0:T(2,128)} %param.26) | copy-start | bytes 12292
  121.7 27.5 %all-to-all-start = ((f32[128,1,224]{2,1,0:T(1,128)}), f32[128,1,224]{2,1,0:T(1,128)S(1)}, u32[]{:S(2)}, u32[]{:S(2)}) async-start(f32[128,1,224]{2,1,0:T(1,128)} %reshape.221), calls=%async_computation | async-start | bytes 262144 | tf_op jit(solution)/shard_map/all_to_all | solution.py:122
  152.1 5.0 %collective-permute-start.4 = (f32[2,28,1]{1,0,2:T(2,128)S(1)}, f32[2,28,1]{1,0,2:T(2,128)S(1)}, u32[]{:S(2)}, u32[]{:S(2)}) collective-permute-start(f32[2,28,1]{1,0,2:T(2,128)S(1)} %get-tuple-element.66), channel_id=1, source_target_pairs={{0,4},{4,8},{8,12},{12,16},{16,20},{20,24},{24,28},{28,32},{32,36}... | collective-permute-start | bytes 680 | tf_op jit(solution)/shard_map/ppermute | solution.py:23
  154.8 4.9 %collective-permute-start.5 = (f32[2,28,1]{1,0,2:T(2,128)S(1)}, f32[2,28,1]{1,0,2:T(2,128)S(1)}, u32[]{:S(2)}, u32[]{:S(2)}) collective-permute-start(f32[2,28,1]{1,0,2:T(2,128)S(1)} %get-tuple-element.67), channel_id=1, source_target_pairs={{4,0},{8,4},{12,8},{16,12},{20,16},{24,20},{28,24},{32,28},{36,32}... | collective-permute-start | bytes 680 | tf_op jit(solution)/shard_map/ppermute | solution.py:24
  161.5 4.7 %collective-permute-start.6 = (f32[2,28,1]{1,0,2:T(2,128)S(1)}, f32[2,28,1]{1,0,2:T(2,128)S(1)}, u32[]{:S(2)}, u32[]{:S(2)}) collective-permute-start(f32[2,28,1]{1,0,2:T(2,128)S(1)} %get-tuple-element.64), channel_id=1, source_target_pairs={{0,4},{4,8},{8,12},{12,16},{16,20},{20,24},{24,28},{28,32},{32,36}... | collective-permute-start | bytes 680 | tf_op jit(solution)/shard_map/ppermute | solution.py:23
  163.5 4.9 %collective-permute-start.7 = (f32[2,28,1]{1,0,2:T(2,128)S(1)}, f32[2,28,1]{1,0,2:T(2,128)S(1)}, u32[]{:S(2)}, u32[]{:S(2)}) collective-permute-start(f32[2,28,1]{1,0,2:T(2,128)S(1)} %get-tuple-element.65), channel_id=1, source_target_pairs={{4,0},{8,4},{12,8},{16,12},{20,16},{24,20},{28,24},{32,28},{36,32}... | collective-permute-start | bytes 680 | tf_op jit(solution)/shard_map/ppermute | solution.py:24
  171.2 4.3 %collective-permute-start.8 = (f32[2,28,1]{1,0,2:T(2,128)S(1)}, f32[2,28,1]{1,0,2:T(2,128)S(1)}, u32[]{:S(2)}, u32[]{:S(2)}) collective-permute-start(f32[2,28,1]{1,0,2:T(2,128)S(1)} %get-tuple-element.62), channel_id=1, source_target_pairs={{0,4},{4,8},{8,12},{12,16},{16,20},{20,24},{24,28},{28,32},{32,36}... | collective-permute-start | bytes 680 | tf_op jit(solution)/shard_map/ppermute | solution.py:23
  173.2 4.9 %collective-permute-start.9 = (f32[2,28,1]{1,0,2:T(2,128)S(1)}, f32[2,28,1]{1,0,2:T(2,128)S(1)}, u32[]{:S(2)}, u32[]{:S(2)}) collective-permute-start(f32[2,28,1]{1,0,2:T(2,128)S(1)} %get-tuple-element.63), channel_id=1, source_target_pairs={{4,0},{8,4},{12,8},{16,12},{20,16},{24,20},{28,24},{32,28},{36,32}... | collective-permute-start | bytes 680 | tf_op jit(solution)/shard_map/ppermute | solution.py:24
  179.9 4.3 %collective-permute-start.10 = (f32[2,28,1]{1,0,2:T(2,128)S(1)}, f32[2,28,1]{1,0,2:T(2,128)S(1)}, u32[]{:S(2)}, u32[]{:S(2)}) collective-permute-start(f32[2,28,1]{1,0,2:T(2,128)S(1)} %get-tuple-element.60), channel_id=1, source_target_pairs={{0,4},{4,8},{8,12},{12,16},{16,20},{20,24},{24,28},{28,32},{32,36}... | collective-permute-start | bytes 680 | tf_op jit(solution)/shard_map/ppermute | solution.py:23
  181.8 4.9 %collective-permute-start.11 = (f32[2,28,1]{1,0,2:T(2,128)S(1)}, f32[2,28,1]{1,0,2:T(2,128)S(1)}, u32[]{:S(2)}, u32[]{:S(2)}) collective-permute-start(f32[2,28,1]{1,0,2:T(2,128)S(1)} %get-tuple-element.61), channel_id=1, source_target_pairs={{4,0},{8,4},{12,8},{16,12},{20,16},{24,20},{28,24},{32,28},{36,32}... | collective-permute-start | bytes 680 | tf_op jit(solution)/shard_map/ppermute | solution.py:24
  188.5 4.5 %collective-permute-start.12 = (f32[2,28,1]{1,0,2:T(2,128)S(1)}, f32[2,28,1]{1,0,2:T(2,128)S(1)}, u32[]{:S(2)}, u32[]{:S(2)}) collective-permute-start(f32[2,28,1]{1,0,2:T(2,128)S(1)} %get-tuple-element.58), channel_id=1, source_target_pairs={{0,4},{4,8},{8,12},{12,16},{16,20},{20,24},{24,28},{28,32},{32,36}... | collective-permute-start | bytes 680 | tf_op jit(solution)/shard_map/ppermute | solution.py:23
  190.5 32.2 %copy-start.1 = (f32[2,28,512]{2,0,1:T(2,128)S(1)}, f32[2,28,512]{2,0,1:T(2,128)}, u32[]{:S(2)}) copy-start(f32[2,28,512]{2,0,1:T(2,128)} %param.20) | copy-start | bytes 344068
  190.5 5.0 %collective-permute-start.13 = (f32[2,28,1]{1,0,2:T(2,128)S(1)}, f32[2,28,1]{1,0,2:T(2,128)S(1)}, u32[]{:S(2)}, u32[]{:S(2)}) collective-permute-start(f32[2,28,1]{1,0,2:T(2,128)S(1)} %get-tuple-element.59), channel_id=1, source_target_pairs={{4,0},{8,4},{12,8},{16,12},{20,16},{24,20},{28,24},{32,28},{36,32}... | collective-permute-start | bytes 680 | tf_op jit(solution)/shard_map/ppermute | solution.py:24
  200.0 35.5 %all-to-all-start.1 = ((f32[128,1,224]{2,1,0:T(1,128)}), f32[128,1,224]{2,1,0:T(1,128)S(1)}, u32[]{:S(2)}, u32[]{:S(2)}) async-start(f32[128,1,224]{2,1,0:T(1,128)} %reshape.223), calls=%async_computation.1 | async-start | bytes 262144 | tf_op jit(solution)/shard_map/all_to_all | solution.py:131
  (1 other events, 15.0 us)
where the time goes:
time: 253 us; the launch traced here: 252 us
  starting transfers between devices  88.6 us (35%)
  other arithmetic  50.4 us (20%)
  blocking collectives  40.3 us (16%)
  waiting for transfers between devices  38.5 us (15%)
  local copies, waits for them, and re-layouts  31 us (12%)
    scatter-add x1, other arithmetic, shards(): jnp.zeros((comps, NFD, faces + 2 * faces), jnp.float32).at[:, :, flat_ids]  32.8 us
    all_to_all x1, starting transfers between devices, shards(): lax.all_to_all(correction, 'dom', split_axis=2, concat_axis=2, tiled=True)  22.7 us
    ppermute x2, starting transfers between devices, passed_along(): return lax.ppermute(block, axis, route)  18.1 us
    ppermute x6, starting transfers between devices, extended_2(): after = lax.ppermute(leading, axis, down)  17.8 us
    ppermute x6, starting transfers between devices, extended_2(): before = lax.ppermute(last, axis, up)  15.2 us
    all_to_all x1, starting transfers between devices, shards(): lax.all_to_all(sendable, 'dom', split_axis=2, concat_axis=2, tiled=True)  14.8 us
    scatter x1, local copies, waits for them, and re-layouts, shards(): owner_order = jnp.zeros_like(returned).at[:, :, solver_slots].set(returned)  13.6 us
    all_to_all x1, waiting for transfers between devices, shards(): lax.all_to_all(sendable, 'dom', split_axis=2, concat_axis=2, tiled=True)  12.5 us
  transfers between devices with their start and end apart: 16, of which 8 were waited for; matrix products, arithmetic and copies ran while one was open for 2% of the time, Pallas kernels for 0%

commit v1 on v0

v1 whole, which is shorter than its diff:
```python
import functools

import jax
import jax.numpy as jnp
from jax import lax
from jax.experimental import pallas as pl
from jax.experimental.pallas import tpu as pltpu
from jax.sharding import PartitionSpec as P

F32 = jnp.float32
BF = jnp.bfloat16
I32 = jnp.int32
MESH = pl.DeviceIdType.MESH

NFD = 28
NID = 84
ND = 128
NF = 4
FACES = 512
ELEMS = 256
CK = 64
EXT = 768
RHO0 = 0.8
HALF = 0.8
RATIO = 1.25


def dot(a, b):
    return jnp.dot(a, b, preferred_element_type=F32)


def dot_nt(a, b):
    return lax.dot_general(a, b, (((1,), (1,)), ((), ())), preferred_element_type=F32)


def iota(shape, dim):
    return lax.broadcasted_iota(I32, shape, dim)


def one_hot(cond):
    return jnp.where(cond, 1.0, 0.0).astype(BF)


def hi_lo(x):
    hi = x.astype(BF)
    lo = (x - hi.astype(F32)).astype(BF)
    return jnp.concatenate([hi, lo], axis=0)


def kernel(
    tr_ref, src_ref, ord_ref, scl_ref, fac_ref, slot_ref, dia_ref, mix_ref,
    ci_hbm, li_hbm, tb_hbm, co_hbm,
    new_ref, mixed_ref,
    ta, oh, gat, civ, liv, tbv, cov, cip, lip, tbp, cop, srcf,
    lo_all, in_all, ra, xn, xp, rims, vb, ln, rn, ll, rr,
    s1, r1, r2, r3, dt, dwin, pm, own32, tbg, ownres,
    wsem, ssem, rsem,
):
    d = lax.axis_index("dom")
    f = lax.axis_index("field")
    z = d // 16
    y = (d % 16) // 2
    k = d % 2

    def dom_at(step):
        return (d + step + ND) % ND

    def field_at(step):
        return (f + step) % NF

    loads_w = []
    for i, (src, dst) in enumerate(((ci_hbm, civ), (tb_hbm, tbv), (li_hbm, liv), (co_hbm, cov))):
        c = pltpu.make_async_copy(src, dst, wsem.at[i])
        c.start()
        loads_w.append(c)

    field_peers = [(d, field_at(i)) for i in range(1, NF)]
    next_all = [(dom_at(1), field_at(i)) for i in range(NF)]
    prev_all = [(dom_at(-1), field_at(i)) for i in range(NF)]
    far = [(dom_at(2), f), (dom_at(-2), f)]
    z_peers = [(((z + i) % 8) * 16 + d % 16, f) for i in range(1, 8)]
    y_peers = [(z * 16 + ((y + i) % 8) * 2 + k, f) for i in range(1, 8)]
    core_peer = (d + 1 - 2 * k, f)
    greet = field_peers + next_all + prev_all + far + z_peers + y_peers
    barrier = pltpu.get_barrier_semaphore()
    for dev in greet:
        pl.semaphore_signal(barrier, inc=1, device_id=dev, device_id_type=MESH)

    count = [0]
    sent = []

    def send(src, dst, dev):
        n = count[0]
        count[0] += 1
        c = pltpu.make_async_remote_copy(
            src_ref=src, dst_ref=dst, send_sem=ssem.at[n], recv_sem=rsem.at[n],
            device_id=dev, device_id_type=MESH,
        )
        c.start()
        sent.append(c)
        return c

    pad16 = jnp.zeros((16, ELEMS), BF)
    for g in range(NF):
        lo_all[g, 176:192, :] = pad16
        in_all[g, 176:192, :] = pad16

    own32[...] = jnp.zeros((CK, FACES), F32)
    for c in range(2):
        own32[c * 32 : c * 32 + NFD, :] = tr_ref[:, c, :]
    ta[f, :, 0:FACES] = own32[...].astype(BF)
    dia = jnp.concatenate([dia_ref[...]] * 4, axis=0)
    for zz in range(8):
        s1[zz] = pltpu.roll(dia, (8 - 64 * zz) % FACES, 1)[0:2, 0:128]

    pl.semaphore_wait(barrier, len(greet))

    ex1 = []
    for dev in next_all:
        ex1.append(send(ta.at[f, :, pl.ds(384, 128)], ta.at[f, :, pl.ds(512, 128)], dev))
    for dev in prev_all:
        ex1.append(send(ta.at[f, :, pl.ds(0, 128)], ta.at[f, :, pl.ds(640, 128)], dev))
    for dev in field_peers:
        ex1.append(send(ta.at[f, :, pl.ds(0, FACES)], ta.at[f, :, pl.ds(0, FACES)], dev))
    dz = []
    for i in range(1, 8):
        dz.append(send(s1.at[(z + i) % 8], r1.at[z], z_peers[i - 1]))
    r1[z] = s1[z]

    rel = (fac_ref[...] - d * FACES) & (ND * FACES - 1)
    lid = jnp.where(
        rel < FACES, rel, jnp.where(rel >= ND * FACES - 128, rel - (ND * FACES - 128) + 512, rel + 128)
    )
    for j in range(4):
        oh[:, j * 256 : (j + 1) * 256] = one_hot(iota((EXT, ELEMS), 0) == lid[j : j + 1, :])
    order = ord_ref[...]
    face_n = (order + 1) * (order + 2)
    inner_n = face_n * (order + 3)
    face_live = 2 * (iota((256, ELEMS), 0) & 31) < face_n
    row = iota((2 * NID, ELEMS), 0)
    inner_live = 6 * jnp.where(row >= NID, row - NID, row) < inner_n
    for c in range(2):
        srcf[c * NID : (c + 1) * NID, :] = src_ref[:, c, :].astype(F32)
    zero8 = jnp.zeros((8, ELEMS), F32)

    col = iota((896, 1024), 1)
    kk = col & 31
    want = jnp.where(kk < NFD, ((col >> 5) & 7) * 112 + (col >> 8) * NFD + kk, -1)
    permk = one_hot(iota((896, 1024), 0) == want)
    loads_w[0].wait()
    cip[...] = dot(civ[...], permk).astype(BF)
    rown = iota((256, 224), 0)
    rk = rown & 31
    want_r = jnp.where(rk < NFD, ((rown >> 5) & 1) * 112 + (rown >> 6) * NFD + rk, -1)
    permr = one_hot(iota((256, 224), 1) == want_r)
    loads_w[1].wait()
    tbp[...] = dot(dot(permr, tbv[...]).astype(BF), permk).astype(BF)

    for c in ex1:
        c.wait_recv()
    tall = ta[...].reshape(256, EXT)
    for j in range(4):
        picked = dot(tall, oh[:, j * 256 : (j + 1) * 256])
        gat[j * 256 : (j + 1) * 256, :] = jnp.where(face_live, picked, 0.0).astype(BF)
    loads = srcf[...] - dot(cip[...], gat[...])
    loads = jnp.where(inner_live, loads, 0.0)
    lo_all[f, 0:176] = jnp.concatenate([loads, zero8], axis=0).astype(BF)

    ex2 = [send(lo_all.at[f, pl.ds(0, 176)], lo_all.at[f, pl.ds(0, 176)], dev) for dev in field_peers]
    for c in dz:
        c.wait_recv()
    for c in range(2):
        r2[y, c] = r1[:, c, :]
    dy = []
    for i in range(1, 8):
        dy.append(send(r2.at[y], r2.at[y], y_peers[i - 1]))

    colw = iota((672, EXT), 1)
    slab = (colw >= 192).astype(I32) + (colw >= 384).astype(I32) + (colw >= 576).astype(I32)
    inn = colw - slab * 192
    perms = one_hot(iota((672, EXT), 0) == jnp.where(inn < 168, slab * 168 + inn, -1))
    loads_w[2].wait()
    lip[...] = dot(liv[...], perms).astype(BF)
    loads_w[3].wait()
    cop[...] = dot(dot(permr, cov[...]).astype(BF), perms).astype(BF)
    tbg[...] = dot(tbp[...], gat[...])

    for c in ex2:
        c.wait_recv()
    inter = dot(lip[...], lo_all[...].reshape(EXT, ELEMS))
    inter = jnp.where(inner_live, inter, 0.0)
    in_all[f, 0:176] = jnp.concatenate([inter, zero8], axis=0).astype(BF)

    ex3 = [send(in_all.at[f, pl.ds(0, 176)], in_all.at[f, pl.ds(0, 176)], dev) for dev in field_peers]
    for c in dy:
        c.wait_recv()
    dk = send(r2, r3.at[k], core_peer)
    r3[k] = r2[...]

    slots = slot_ref[...]
    parts = jnp.concatenate([(slots >> 4).astype(F32), (slots & 15).astype(F32)] + [jnp.zeros((6, FACES), F32)], axis=0)
    cs = iota((FACES, FACES), 1)
    spread = one_hot(iota((FACES, FACES), 0) == (cs & 127) * 4 + (cs >> 7))
    moved = dot(parts.astype(BF), spread).astype(I32)
    slot_qt = moved[0:1] * 16 + moved[1:2]
    pm[...] = one_hot(iota((FACES, FACES), 0) == slot_qt)

    for c in ex3:
        c.wait_recv()
    blocks = tbg[...] + dot(cop[...], in_all[...].reshape(EXT, ELEMS))
    blocks = jnp.where(face_live, blocks, 0.0) * scl_ref[...]
    acc = jnp.zeros((2 * CK, EXT), F32)
    for j in range(4):
        acc = acc + dot_nt(hi_lo(blocks[j * CK : (j + 1) * CK]), oh[:, j * 256 : (j + 1) * 256])
    res = acc[0:CK] + acc[CK : 2 * CK]
    ownres[...] = res[:, 0:FACES]
    rims[0] = res[:, 512:640].astype(BF)
    rims[1] = res[:, 640:768].astype(BF)
    ra[f] = res[:, 0:FACES].astype(BF)

    ex4 = []
    for dev in prev_all:
        ex4.append(send(rims.at[0], xn.at[f], dev))
    for dev in next_all:
        ex4.append(send(rims.at[1], xp.at[f], dev))
    for dev in field_peers:
        ex4.append(send(ra.at[f], ra.at[f], dev))

    dk.wait_recv()
    r_i = iota((128, 128), 0)
    t_of = (r_i & 7) * 16 + ((r_i >> 3) & 7) * 2 + (r_i >> 6)
    to_t = one_hot(iota((128, 128), 1) == t_of)
    for c in range(2):
        dt[c] = r3[:, :, c].reshape(128, 128).T
    start = 3 + 4 * (d % 16)
    lane = iota((1, 128), 1)
    for c in range(2):
        win = dt[c, pl.ds(start, 16), :]
        w0 = win.astype(BF)
        rest = win - w0.astype(F32)
        w1 = rest.astype(BF)
        w2 = (rest - w1.astype(F32)).astype(BF)
        got = dot(jnp.concatenate([w0, w1, w2], axis=0), to_t)
        dwin[c] = 1.0 / (got[0:16] + got[16:32] + got[32:48])

    def shifted(v, wrap, step):
        edge = 0 if step == 1 else 127
        rolled = jnp.where(lane == edge, 0.0, pltpu.roll(v, step % 128, 1))
        return jnp.where(wrap, rolled, v)

    wraps = [d <= 1] + [d == 0] * 4 + [None] * 4 + [d == ND - 1] * 4 + [d >= ND - 2]

    def placed(v, i):
        if i < 5:
            return shifted(v, wraps[i], 1)
        if i > 8:
            return shifted(v, wraps[i], -1)
        return v

    inv = []
    for c in range(2):
        inv.append([placed(jnp.broadcast_to(dwin[c, i : i + 1, :], (8, 128)), i) for i in range(14)])

    for c in ex4:
        c.wait_recv()

    mine = ownres[...]
    first_rim = xp[...].astype(F32)
    last_rim = xn[...].astype(F32)
    mixed = [None, None]
    for g in range(NF):
        whole = jnp.where(f == g, mine, ra[g].astype(F32))
        whole = jnp.concatenate(
            [whole[:, 0:128] + first_rim[g], whole[:, 128:384], whole[:, 384:512] + last_rim[g]], axis=1
        )
        for cc in range(2):
            part = whole[cc * 32 : cc * 32 + 32]
            for c in range(2):
                coef = mix_ref[c : c + 1, 2 * g + cc : 2 * g + cc + 1]
                coef = coef + jnp.where((f == g) & (c == cc), 1.0, 0.0)
                term = coef * part
                mixed[c] = term if mixed[c] is None else mixed[c] + term
    both = jnp.concatenate(mixed, axis=0)
    moved_rhs = dot(hi_lo(both), pm[...])
    rhs = moved_rhs[0:CK] + moved_rhs[CK : 2 * CK]
    vb[...] = rhs.astype(BF)

    ex5 = [
        send(vb, ln, (dom_at(1), f)),
        send(vb, rn, (dom_at(-1), f)),
        send(vb.at[:, pl.ds(384, 128)], ll, far[0]),
        send(vb.at[:, pl.ds(0, 128)], rr, far[1]),
    ]
    for c in range(2):
        mixed_ref[c] = mixed[c][0:NFD]
    for c in ex5:
        c.wait_recv()

    corr = []
    for b in range(8):
        rows = slice(b * 8, b * 8 + 8)
        iv = inv[b // 4]
        pair = slice((b // 2) * 16, (b // 2) * 16 + 16)
        half = slice((b % 2) * 8, (b % 2) * 8 + 8)

        def get(ref, q):
            return ref[pair, q * 128 : (q + 1) * 128].astype(F32)[half]

        r = [get(ll, 0)] + [get(ln, q) for q in range(4)] + [rhs[rows, q * 128 : (q + 1) * 128] for q in range(4)]
        r = r + [get(rn, q) for q in range(4)] + [get(rr, 0)]
        yv = {i: iv[i] * placed(r[i], i) for i in range(14)}

        def residual(yy, zz, lo, hi):
            return {i: yy[i] + iv[i] * (zz[i - 1] + zz[i + 1]) - zz[i] for i in range(lo, hi)}

        def sweep(yy, lo, hi):
            step = dict(yy)
            total = dict(yy)
            rho = RHO0
            for _ in range(2):
                lo, hi = lo + 1, hi - 1
                rho_next = 1.0 / (2.0 * RATIO - rho)
                u = residual(yy, total, lo, hi)
                step = {i: (rho_next * rho) * step[i] + (2.0 * rho_next / HALF) * u[i] for i in range(lo, hi)}
                total = {i: total[i] + step[i] for i in range(lo, hi)}
                rho = rho_next
            return total, lo, hi

        first, lo, hi = sweep(yv, 0, 14)
        y2 = residual(yv, first, lo + 1, hi - 1)
        second, lo, hi = sweep(y2, lo + 1, hi - 1)
        corr.append(jnp.concatenate([first[i] + second[i] for i in range(5, 9)], axis=1))
    corr = jnp.concatenate(corr, axis=0)
    back = dot_nt(hi_lo(corr), pm[...])
    new = own32[...] - (back[0:CK] + back[CK : 2 * CK])
    for c in range(2):
        new_ref[c] = new[c * 32 : c * 32 + NFD]
    for c in sent:
        c.wait_send()


def shards(
    traces,
    interior_source,
    orders,
    element_scale,
    element_faces,
    solver_slots,
    line_diagonal,
    species_mix,
    couple_in,
    local_inverse,
    trace_block,
    couple_out,
):
    vmem = pl.BlockSpec(memory_space=pltpu.VMEM)
    anyw = pl.BlockSpec(memory_space=pl.ANY)
    n_copies = 64
    scratch = [
        pltpu.VMEM((NF, CK, EXT), BF),
        pltpu.VMEM((EXT, 1024), BF),
        pltpu.VMEM((1024, ELEMS), BF),
        pltpu.VMEM((168, 896), BF),
        pltpu.VMEM((168, 672), BF),
        pltpu.VMEM((224, 896), BF),
        pltpu.VMEM((224, 672), BF),
        pltpu.VMEM((168, 1024), BF),
        pltpu.VMEM((168, EXT), BF),
        pltpu.VMEM((256, 1024), BF),
        pltpu.VMEM((256, EXT), BF),
        pltpu.VMEM((168, ELEMS), F32),
        pltpu.VMEM((NF, 192, ELEMS), BF),
        pltpu.VMEM((NF, 192, ELEMS), BF),
        pltpu.VMEM((NF, CK, FACES), BF),
        pltpu.VMEM((NF, CK, 128), BF),
        pltpu.VMEM((NF, CK, 128), BF),
        pltpu.VMEM((2, CK, 128), BF),
        pltpu.VMEM((CK, FACES), BF),
        pltpu.VMEM((CK, FACES), BF),
        pltpu.VMEM((CK, FACES), BF),
        pltpu.VMEM((CK, 128), BF),
        pltpu.VMEM((CK, 128), BF),
        pltpu.VMEM((8, 2, 128), F32),
        pltpu.VMEM((8, 2, 128), F32),
        pltpu.VMEM((8, 2, 8, 128), F32),
        pltpu.VMEM((2, 8, 2, 8, 128), F32),
        pltpu.VMEM((2, 128, 128), F32),
        pltpu.VMEM((2, 16, 128), F32),
        pltpu.VMEM((FACES, FACES), BF),
        pltpu.VMEM((CK, FACES), F32),
        pltpu.VMEM((256, ELEMS), F32),
        pltpu.VMEM((CK, FACES), F32),
        pltpu.SemaphoreType.DMA((4,)),
        pltpu.SemaphoreType.DMA((n_copies,)),
        pltpu.SemaphoreType.DMA((n_copies,)),
    ]
    shape = jax.ShapeDtypeStruct((2, NFD, FACES), F32)
    new, mixed = pl.pallas_call(
        kernel,
        out_shape=(shape, shape),
        in_specs=[vmem] * 8 + [anyw] * 4,
        out_specs=(vmem, vmem),
        scratch_shapes=scratch,
        compiler_params=pltpu.CompilerParams(
            collective_id=0, has_side_effects=True, vmem_limit_bytes=48 * 1024 * 1024
        ),
    )(
        jnp.transpose(traces, (1, 0, 2)),
        jnp.transpose(interior_source, (1, 0, 2)),
        orders.reshape(1, ELEMS),
        element_scale.reshape(1, ELEMS),
        element_faces,
        solver_slots.reshape(1, FACES),
        line_diagonal,
        species_mix,
        couple_in,
        local_inverse,
        trace_block,
        couple_out,
    )
    return new, mixed


def solution(mesh):
    in_specs = (
        P("field", None, "dom"),
        P("field", None, "dom"),
        P("dom"),
        P("dom"),
        P(None, "dom"),
        P("dom"),
        P("field", "dom"),
        P("field", None),
        P("field", None),
        P("field", None),
        P("field", None),
        P("field", None),
    )
    out_specs = (P("field", None, "dom"), P("field", None, "dom"))
    return jax.shard_map(shards, mesh=mesh, in_specs=in_specs, out_specs=out_specs, check_vma=False)
```

time: 253 us -> 58.7 us (0.23)
  starting transfers between devices: 88.6 us -> 0 us
  other arithmetic: 50.4 us -> 0 us
  Pallas kernels: 0 us -> 47.8 us
  blocking collectives: 40.3 us -> 0 us
  waiting for transfers between devices: 38.5 us -> 0 us
  local copies, waits for them, and re-layouts: 31 us -> 9.87 us
    ppermute x14 -> x0, starting transfers between devices: 51.1 us -> none  [the longest x2 18.1 us: passed_along(): return lax.ppermute(block, axis, route)]
    pallas_call x0 -> x1, Pallas kernels: none -> 47.8 us  [shards(): pl.pallas_call(kernel, out_shape=(shape, shape), in_specs=[vmem] * 8 + [a...]
    all_gather x4 -> x0, blocking collectives: 40.3 us -> none  [the longest x1 10.7 us: shards(): interior_all = lax.all_gather(interior_own, 'field', axis=0, tiled=True)]
    all_to_all x2 -> x0, starting transfers between devices: 37.5 us -> none  [the longest x1 22.7 us: shards(): lax.all_to_all(correction, 'dom', split_axis=2, concat_axis=2, tiled=True)]
    scatter-add x1 -> x0, other arithmetic: 32.8 us -> none  [shards(): jnp.zeros((comps, NFD, faces + 2 * faces), jnp.float32).at[:, :, flat_ids]]
    all_to_all x2 -> x0, waiting for transfers between devices: 25 us -> none  [the longest x1 12.5 us: shards(): lax.all_to_all(sendable, 'dom', split_axis=2, concat_axis=2, tiled=True)]
    scatter x1 -> x0, local copies, waits for them, and re-layouts: 13.6 us -> none  [shards(): owner_order = jnp.zeros_like(returned).at[:, :, solver_slots].set(returned)]
    ppermute x14 -> x0, waiting for transfers between devices: 13.5 us -> none  [the longest x6 12.3 us: extended_2(): after = lax.ppermute(leading, axis, down)]
  transfers between devices with their start and end apart: 16 -> 0, of which waited for: 8 -> 0; matrix products, arithmetic and copies ran while one was open for 2% -> 0% of each run, Pallas kernels for 0% -> 0%
where the time goes in v1:
time: 58.7 us; the launch traced here: 58.3 us
  Pallas kernels  47.8 us (81%)
  local copies, waits for them, and re-layouts  9.87 us (17%)
  between operations  0.68 us (1%)
    pallas_call x1, Pallas kernels, shards(): pl.pallas_call(kernel, out_shape=(shape, shape), in_specs=[vmem] * 8 + [a...  47.8 us
    unnamed x24, local copies, waits for them, and re-layouts  8.4 us
    pallas_call x2, local copies, waits for them, and re-layouts, shards(): pl.pallas_call(kernel, out_shape=(shape, shape), in_specs=[vmem] * 8 + [a...  1.47 us

profile of v1, /device:TPU:1, one launch (start us, length us, event | category | flops | bytes accessed | tf_op | source)
XLA Modules:
  0.0 58.3 jit_solution(5426012319795952149)
XLA Ops:
  0.6 0.0 copy-start.7
  0.6 0.0 copy-start.6
  0.7 0.0 copy-start.9
  0.7 0.7 %copy-done.7 = f32[2,512]{1,0:T(2,128)S(1)} copy-done((f32[2,512]{1,0:T(2,128)S(1)}, f32[2,512]{1,0:T(2,128)}, u32[]{:S(2)}) %copy-start.7) | copy-done | bytes 4120
  1.3 0.0 copy-done.6
  1.3 0.0 copy-done.9
  1.3 0.0 copy-start
  1.3 1.0 %copy-done = bf16[224,896]{1,0:T(8,128)(2,1)S(1)} copy-done((bf16[224,896]{1,0:T(8,128)(2,1)S(1)}, bf16[224,896]{1,0:T(8,128)(2,1)}, u32[]{:S(2)}) %copy-start) | copy-done | bytes 401432
  2.3 0.0 copy-start.1
  2.3 1.0 %copy-done.1 = bf16[224,672]{1,0:T(8,128)(2,1)S(1)} copy-done((bf16[224,672]{1,0:T(8,128)(2,1)S(1)}, bf16[224,672]{1,0:T(8,128)(2,1)}, u32[]{:S(2)}) %copy-start.1) | copy-done | bytes 301080
  3.3 0.0 copy-start.2
  3.3 1.0 %copy-done.2 = bf16[168,896]{1,0:T(8,128)(2,1)S(1)} copy-done((bf16[168,896]{1,0:T(8,128)(2,1)S(1)}, bf16[168,896]{1,0:T(8,128)(2,1)}, u32[]{:S(2)}) %copy-start.2) | copy-done | bytes 301080
  4.3 0.0 copy-start.3
  4.3 0.9 %copy-done.3 = bf16[168,672]{1,0:T(8,128)(2,1)S(1)} copy-done((bf16[168,672]{1,0:T(8,128)(2,1)S(1)}, bf16[168,672]{1,0:T(8,128)(2,1)}, u32[]{:S(2)}) %copy-start.3) | copy-done | bytes 225816
  5.2 0.0 copy-start.4
  5.2 0.9 %copy-done.4 = f32[2,28,512]{2,0,1:T(2,128)S(1)} copy-done((f32[2,28,512]{2,0,1:T(2,128)S(1)}, f32[2,28,512]{2,0,1:T(2,128)}, u32[]{:S(2)}) %copy-start.4) | copy-done | bytes 114712
  6.1 0.0 copy-start.5
  6.1 0.9 %copy-done.5 = bf16[2,84,256]{2,0,1:T(2,128)(2,1)S(1)} copy-done((bf16[2,84,256]{2,0,1:T(2,128)(2,1)S(1)}, bf16[2,84,256]{2,0,1:T(2,128)(2,1)}, u32[]{:S(2)}) %copy-start.5) | copy-done | bytes 86040
  7.0 0.7 %copy-done.8 = s32[512]{0:T(512)S(1)} copy-done((s32[512]{0:T(512)S(1)}, s32[512]{0:T(512)}, u32[]{:S(2)}) %copy-start.8) | copy-done | bytes 2072
  7.7 0.7 %copy-done.10 = f32[256]{0:T(256)S(1)} copy-done((f32[256]{0:T(256)S(1)}, f32[256]{0:T(256)}, u32[]{:S(2)}) %copy-start.10) | copy-done | bytes 1048
  8.4 0.7 %copy-done.11 = f32[2,8]{1,0:T(2,128)S(1)} copy-done((f32[2,8]{1,0:T(2,128)S(1)}, f32[2,8]{1,0:T(2,128)}, u32[]{:S(2)}) %copy-start.11) | copy-done | bytes 88
  9.1 47.8 %shard_map.131 = (f32[2,28,512]{2,1,0:T(8,128)S(1)}, f32[2,28,512]{2,1,0:T(8,128)S(1)}) custom-call(f32[28,2,512]{2,1,0:T(2,128)S(1)} %bitcast.5, bf16[84,2,256]{2,1,0:T(2,128)(2,1)S(1)} %bitcast.6, s32[1,256]{1,0:T(1,128)S(1)} %bitcast.8, f32[1,256]{1,0:T(1,128)S(1)} %bitcast.9, s32[4,256]{1,0:T(4,128)S(1)} %copy-done.6, s32[1,512]{1,0:T(1,128)S(1)} %bitcast.7, ...), custom_call_target="tpu_custom_call" | custom-call | tf_op jit(solution)/shard_map/pallas_call | solution.py:398
  56.9 0.7 %copy.14 = f32[2,28,512]{2,0,1:T(2,128)} copy(f32[2,28,512]{2,1,0:T(8,128)S(1)} %get-tuple-element.2) | data formatting | bytes 229376 | tf_op jit(solution)/shard_map/pallas_call | solution.py:398
  57.6 0.7 %copy.15 = f32[2,28,512]{2,0,1:T(2,128)} copy(f32[2,28,512]{2,1,0:T(8,128)S(1)} %get-tuple-element.3) | data formatting | bytes 229376 | tf_op jit(solution)/shard_map/pallas_call | solution.py:398
  (3 shorter events, 0.0 us)
Async XLA Ops:
  0.6 0.7 %copy-start.7 = (f32[2,512]{1,0:T(2,128)S(1)}, f32[2,512]{1,0:T(2,128)}, u32[]{:S(2)}) copy-start(f32[2,512]{1,0:T(2,128)} %dia_ref.1) | copy-start | bytes 12292
  0.6 0.7 %copy-start.6 = (s32[4,256]{1,0:T(4,128)S(1)}, s32[4,256]{1,0:T(4,128)}, u32[]{:S(2)}) copy-start(s32[4,256]{1,0:T(4,128)} %fac_ref.1) | copy-start | bytes 12292
  0.7 0.7 %copy-start.9 = (s32[256]{0:T(256)S(1)}, s32[256]{0:T(256)}, u32[]{:S(2)}) copy-start(s32[256]{0:T(256)} %param.14) | copy-start | bytes 3076
  1.3 1.0 %copy-start = (bf16[224,896]{1,0:T(8,128)(2,1)S(1)}, bf16[224,896]{1,0:T(8,128)(2,1)}, u32[]{:S(2)}) copy-start(bf16[224,896]{1,0:T(8,128)(2,1)} %tb_hbm.1) | copy-start | bytes 1204228
  2.3 1.0 %copy-start.1 = (bf16[224,672]{1,0:T(8,128)(2,1)S(1)}, bf16[224,672]{1,0:T(8,128)(2,1)}, u32[]{:S(2)}) copy-start(bf16[224,672]{1,0:T(8,128)(2,1)} %co_hbm.1) | copy-start | bytes 903172
  3.3 1.0 %copy-start.2 = (bf16[168,896]{1,0:T(8,128)(2,1)S(1)}, bf16[168,896]{1,0:T(8,128)(2,1)}, u32[]{:S(2)}) copy-start(bf16[168,896]{1,0:T(8,128)(2,1)} %ci_hbm.1) | copy-start | bytes 903172
  4.3 0.9 %copy-start.3 = (bf16[168,672]{1,0:T(8,128)(2,1)S(1)}, bf16[168,672]{1,0:T(8,128)(2,1)}, u32[]{:S(2)}) copy-start(bf16[168,672]{1,0:T(8,128)(2,1)} %li_hbm.1) | copy-start | bytes 677380
  5.2 0.9 %copy-start.4 = (f32[2,28,512]{2,0,1:T(2,128)S(1)}, f32[2,28,512]{2,0,1:T(2,128)}, u32[]{:S(2)}) copy-start(f32[2,28,512]{2,0,1:T(2,128)} %param.12) | copy-start | bytes 344068
  6.1 0.9 %copy-start.5 = (bf16[2,84,256]{2,0,1:T(2,128)(2,1)S(1)}, bf16[2,84,256]{2,0,1:T(2,128)(2,1)}, u32[]{:S(2)}) copy-start(bf16[2,84,256]{2,0,1:T(2,128)(2,1)} %param.13) | copy-start | bytes 258052
  7.0 0.7 %copy-start.8 = (s32[512]{0:T(512)S(1)}, s32[512]{0:T(512)}, u32[]{:S(2)}) copy-start(s32[512]{0:T(512)} %param.17) | copy-start | bytes 6148
  7.7 0.7 %copy-start.10 = (f32[256]{0:T(256)S(1)}, f32[256]{0:T(256)}, u32[]{:S(2)}) copy-start(f32[256]{0:T(256)} %param.15) | copy-start | bytes 3076
  8.4 0.7 %copy-start.11 = (f32[2,8]{1,0:T(2,128)S(1)}, f32[2,8]{1,0:T(2,128)}, u32[]{:S(2)}) copy-start(f32[2,8]{1,0:T(2,128)} %mix_ref.1) | copy-start | bytes 196

commit v2 on v1

--- a/solution.py
+++ b/solution.py
@@ -19,7 +19,10 @@
 FACES = 512
 ELEMS = 256
 CK = 64
-EXT = 768
+EXT = 640
+PADK = 768
+HE = 128
+RIM = 32
 RHO0 = 0.8
 HALF = 0.8
 RATIO = 1.25
@@ -47,13 +50,29 @@
     return jnp.concatenate([hi, lo], axis=0)
 
 
+def packed_rim(x, lane0):
+    lane = iota((16, 128), 1)
+    out = jnp.zeros((16, 128), F32)
+    for i in range(4):
+        part = pltpu.roll(x[16 * i : 16 * i + 16], (RIM * i - lane0) % 128, 1)
+        out = jnp.where((lane >= RIM * i) & (lane < RIM * i + RIM), part, out)
+    return out
+
+
+def unpacked_rim(x, lane0):
+    lane = iota((16, 128), 1)
+    keep = (lane >= lane0) & (lane < lane0 + RIM)
+    parts = [jnp.where(keep, pltpu.roll(x, (lane0 - RIM * i) % 128, 1), 0.0) for i in range(4)]
+    return jnp.concatenate(parts, axis=0)
+
+
 def kernel(
-    tr_ref, src_ref, ord_ref, scl_ref, fac_ref, slot_ref, dia_ref, mix_ref,
-    ci_hbm, li_hbm, tb_hbm, co_hbm,
+    dia_hbm, tr_hbm, fac_hbm, ord_hbm, src_hbm, ci_hbm, tb_hbm, li_hbm, co_hbm, slot_hbm, scl_hbm, mix_hbm,
     new_ref, mixed_ref,
     ta, oh, gat, civ, liv, tbv, cov, cip, lip, tbp, cop, srcf,
-    lo_all, in_all, ra, xn, xp, rims, vb, ln, rn, ll, rr,
+    lo_all, in_all, ra, rim1, xr1, rim4, xr4, vb, ln, rn, ll, rr,
     s1, r1, r2, r3, dt, dwin, pm, own32, tbg, ownres,
+    dia_ref, tr_ref, fac_ref, ord_ref, src_ref, slot_ref, scl_ref, mix_ref,
     wsem, ssem, rsem,
 ):
     d = lax.axis_index("dom")
@@ -68,11 +87,14 @@
     def field_at(step):
         return (f + step) % NF
 
-    loads_w = []
-    for i, (src, dst) in enumerate(((ci_hbm, civ), (tb_hbm, tbv), (li_hbm, liv), (co_hbm, cov))):
-        c = pltpu.make_async_copy(src, dst, wsem.at[i])
+    pairs = (
+        (dia_hbm, dia_ref), (tr_hbm, tr_ref), (fac_hbm, fac_ref), (ord_hbm, ord_ref), (src_hbm, src_ref),
+        (ci_hbm, civ), (tb_hbm, tbv), (li_hbm, liv), (co_hbm, cov),
+        (slot_hbm, slot_ref), (scl_hbm, scl_ref), (mix_hbm, mix_ref),
+    )
+    fetch = [pltpu.make_async_copy(src, dst, wsem.at[i]) for i, (src, dst) in enumerate(pairs)]
+    for c in fetch:
         c.start()
-        loads_w.append(c)
 
     field_peers = [(d, field_at(i)) for i in range(1, NF)]
     next_all = [(dom_at(1), field_at(i)) for i in range(NF)]
@@ -100,15 +122,20 @@
         sent.append(c)
         return c
 
-    pad16 = jnp.zeros((16, ELEMS), BF)
+    pad16 = jnp.zeros((16, HE), BF)
     for g in range(NF):
-        lo_all[g, 176:192, :] = pad16
-        in_all[g, 176:192, :] = pad16
+        for h in range(2):
+            lo_all[h, g, 176:192, :] = pad16
+            in_all[h, g, 176:192, :] = pad16
 
     own32[...] = jnp.zeros((CK, FACES), F32)
+    fetch[1].wait()
     for c in range(2):
         own32[c * 32 : c * 32 + NFD, :] = tr_ref[:, c, :]
     ta[f, :, 0:FACES] = own32[...].astype(BF)
+    rim1[0] = packed_rim(own32[:, 0:128], 0).astype(BF)
+    rim1[1] = packed_rim(own32[:, 384:512], 96).astype(BF)
+    fetch[0].wait()
     dia = jnp.concatenate([dia_ref[...]] * 4, axis=0)
     for zz in range(8):
         s1[zz] = pltpu.roll(dia, (8 - 64 * zz) % FACES, 1)[0:2, 0:128]
@@ -117,9 +144,9 @@
 
     ex1 = []
     for dev in next_all:
-        ex1.append(send(ta.at[f, :, pl.ds(384, 128)], ta.at[f, :, pl.ds(512, 128)], dev))
+        ex1.append(send(rim1.at[1], xr1.at[0, f], dev))
     for dev in prev_all:
-        ex1.append(send(ta.at[f, :, pl.ds(0, 128)], ta.at[f, :, pl.ds(640, 128)], dev))
+        ex1.append(send(rim1.at[0], xr1.at[1, f], dev))
     for dev in field_peers:
         ex1.append(send(ta.at[f, :, pl.ds(0, FACES)], ta.at[f, :, pl.ds(0, FACES)], dev))
     dz = []
@@ -127,46 +154,59 @@
         dz.append(send(s1.at[(z + i) % 8], r1.at[z], z_peers[i - 1]))
     r1[z] = s1[z]
 
+    fetch[2].wait()
     rel = (fac_ref[...] - d * FACES) & (ND * FACES - 1)
     lid = jnp.where(
-        rel < FACES, rel, jnp.where(rel >= ND * FACES - 128, rel - (ND * FACES - 128) + 512, rel + 128)
+        rel < FACES, rel, jnp.where(rel >= ND * FACES - RIM, rel - (ND * FACES - RIM) + FACES, rel + RIM)
     )
-    for j in range(4):
-        oh[:, j * 256 : (j + 1) * 256] = one_hot(iota((EXT, ELEMS), 0) == lid[j : j + 1, :])
+    for h in range(2):
+        for j in range(4):
+            c0 = h * 512 + j * HE
+            oh[:, c0 : c0 + HE] = one_hot(iota((EXT, HE), 0) == lid[j : j + 1, h * HE : h * HE + HE])
+    fetch[3].wait()
     order = ord_ref[...]
     face_n = (order + 1) * (order + 2)
     inner_n = face_n * (order + 3)
     face_live = 2 * (iota((256, ELEMS), 0) & 31) < face_n
     row = iota((2 * NID, ELEMS), 0)
     inner_live = 6 * jnp.where(row >= NID, row - NID, row) < inner_n
+    fetch[4].wait()
     for c in range(2):
         srcf[c * NID : (c + 1) * NID, :] = src_ref[:, c, :].astype(F32)
-    zero8 = jnp.zeros((8, ELEMS), F32)
+    zero8 = jnp.zeros((8, HE), F32)
 
     col = iota((896, 1024), 1)
     kk = col & 31
     want = jnp.where(kk < NFD, ((col >> 5) & 7) * 112 + (col >> 8) * NFD + kk, -1)
     permk = one_hot(iota((896, 1024), 0) == want)
-    loads_w[0].wait()
+    fetch[5].wait()
     cip[...] = dot(civ[...], permk).astype(BF)
     rown = iota((256, 224), 0)
     rk = rown & 31
     want_r = jnp.where(rk < NFD, ((rown >> 5) & 1) * 112 + (rown >> 6) * NFD + rk, -1)
     permr = one_hot(iota((256, 224), 1) == want_r)
-    loads_w[1].wait()
+    fetch[6].wait()
     tbp[...] = dot(dot(permr, tbv[...]).astype(BF), permk).astype(BF)
 
     for c in ex1:
         c.wait_recv()
+    for g in range(NF):
+        ta[g, :, FACES:EXT] = (
+            unpacked_rim(xr1[0, g].astype(F32), 0) + unpacked_rim(xr1[1, g].astype(F32), RIM)
+        ).astype(BF)
     tall = ta[...].reshape(256, EXT)
-    for j in range(4):
-        picked = dot(tall, oh[:, j * 256 : (j + 1) * 256])
-        gat[j * 256 : (j + 1) * 256, :] = jnp.where(face_live, picked, 0.0).astype(BF)
-    loads = srcf[...] - dot(cip[...], gat[...])
-    loads = jnp.where(inner_live, loads, 0.0)
-    lo_all[f, 0:176] = jnp.concatenate([loads, zero8], axis=0).astype(BF)
-
-    ex2 = [send(lo_all.at[f, pl.ds(0, 176)], lo_all.at[f, pl.ds(0, 176)], dev) for dev in field_peers]
+    ex2 = [[], []]
+    for h in range(2):
+        es = slice(h * HE, h * HE + HE)
+        picked = dot(tall, oh[:, h * 512 : h * 512 + 512])
+        for j in range(4):
+            live = jnp.where(face_live[:, es], picked[:, j * HE : (j + 1) * HE], 0.0)
+            gat[h, j * 256 : (j + 1) * 256, :] = live.astype(BF)
+        loads = srcf[:, es] - dot(cip[...], gat[h])
+        loads = jnp.where(inner_live[:, es], loads, 0.0)
+        lo_all[h, f, 0:176] = jnp.concatenate([loads, zero8], axis=0).astype(BF)
+        for dev in field_peers:
+            ex2[h].append(send(lo_all.at[h, f, pl.ds(0, 176)], lo_all.at[h, f, pl.ds(0, 176)], dev))
     for c in dz:
         c.wait_recv()
     for c in range(2):
@@ -175,28 +215,33 @@
     for i in range(1, 8):
         dy.append(send(r2.at[y], r2.at[y], y_peers[i - 1]))
 
-    colw = iota((672, EXT), 1)
+    colw = iota((672, PADK), 1)
     slab = (colw >= 192).astype(I32) + (colw >= 384).astype(I32) + (colw >= 576).astype(I32)
     inn = colw - slab * 192
-    perms = one_hot(iota((672, EXT), 0) == jnp.where(inn < 168, slab * 168 + inn, -1))
-    loads_w[2].wait()
+    perms = one_hot(iota((672, PADK), 0) == jnp.where(inn < 168, slab * 168 + inn, -1))
+    fetch[7].wait()
     lip[...] = dot(liv[...], perms).astype(BF)
-    loads_w[3].wait()
+    fetch[8].wait()
     cop[...] = dot(dot(permr, cov[...]).astype(BF), perms).astype(BF)
-    tbg[...] = dot(tbp[...], gat[...])
-
-    for c in ex2:
-        c.wait_recv()
-    inter = dot(lip[...], lo_all[...].reshape(EXT, ELEMS))
-    inter = jnp.where(inner_live, inter, 0.0)
-    in_all[f, 0:176] = jnp.concatenate([inter, zero8], axis=0).astype(BF)
-
-    ex3 = [send(in_all.at[f, pl.ds(0, 176)], in_all.at[f, pl.ds(0, 176)], dev) for dev in field_peers]
+    for h in range(2):
+        tbg[h] = dot(tbp[...], gat[h])
+
+    ex3 = [[], []]
+    for h in range(2):
+        es = slice(h * HE, h * HE + HE)
+        for c in ex2[h]:
+            c.wait_recv()
+        inter = dot(lip[...], lo_all[h].reshape(PADK, HE))
+        inter = jnp.where(inner_live[:, es], inter, 0.0)
+        in_all[h, f, 0:176] = jnp.concatenate([inter, zero8], axis=0).astype(BF)
+        for dev in field_peers:
+            ex3[h].append(send(in_all.at[h, f, pl.ds(0, 176)], in_all.at[h, f, pl.ds(0, 176)], dev))
     for c in dy:
         c.wait_recv()
     dk = send(r2, r3.at[k], core_peer)
     r3[k] = r2[...]
 
+    fetch[9].wait()
     slots = slot_ref[...]
     parts = jnp.concatenate([(slots >> 4).astype(F32), (slots & 15).astype(F32)] + [jnp.zeros((6, FACES), F32)], axis=0)
     cs = iota((FACES, FACES), 1)
@@ -205,24 +250,28 @@
     slot_qt = moved[0:1] * 16 + moved[1:2]
     pm[...] = one_hot(iota((FACES, FACES), 0) == slot_qt)
 
-    for c in ex3:
-        c.wait_recv()
-    blocks = tbg[...] + dot(cop[...], in_all[...].reshape(EXT, ELEMS))
-    blocks = jnp.where(face_live, blocks, 0.0) * scl_ref[...]
+    fetch[10].wait()
+    fetch[11].wait()
     acc = jnp.zeros((2 * CK, EXT), F32)
-    for j in range(4):
-        acc = acc + dot_nt(hi_lo(blocks[j * CK : (j + 1) * CK]), oh[:, j * 256 : (j + 1) * 256])
+    for h in range(2):
+        es = slice(h * HE, h * HE + HE)
+        for c in ex3[h]:
+            c.wait_recv()
+        blocks = tbg[h] + dot(cop[...], in_all[h].reshape(PADK, HE))
+        blocks = jnp.where(face_live[:, es], blocks, 0.0) * scl_ref[:, es]
+        wide = jnp.concatenate([blocks[j * CK : (j + 1) * CK] for j in range(4)], axis=1)
+        acc = acc + dot_nt(hi_lo(wide), oh[:, h * 512 : h * 512 + 512])
     res = acc[0:CK] + acc[CK : 2 * CK]
     ownres[...] = res[:, 0:FACES]
-    rims[0] = res[:, 512:640].astype(BF)
-    rims[1] = res[:, 640:768].astype(BF)
+    rim4[0] = packed_rim(res[:, FACES:EXT], 0).astype(BF)
+    rim4[1] = packed_rim(res[:, FACES:EXT], RIM).astype(BF)
     ra[f] = res[:, 0:FACES].astype(BF)
 
     ex4 = []
     for dev in prev_all:
-        ex4.append(send(rims.at[0], xn.at[f], dev))
+        ex4.append(send(rim4.at[0], xr4.at[0, f], dev))
     for dev in next_all:
-        ex4.append(send(rims.at[1], xp.at[f], dev))
+        ex4.append(send(rim4.at[1], xr4.at[1, f], dev))
     for dev in field_peers:
         ex4.append(send(ra.at[f], ra.at[f], dev))
 
@@ -265,13 +314,16 @@
         c.wait_recv()
 
     mine = ownres[...]
-    first_rim = xp[...].astype(F32)
-    last_rim = xn[...].astype(F32)
     mixed = [None, None]
     for g in range(NF):
         whole = jnp.where(f == g, mine, ra[g].astype(F32))
         whole = jnp.concatenate(
-            [whole[:, 0:128] + first_rim[g], whole[:, 128:384], whole[:, 384:512] + last_rim[g]], axis=1
+            [
+                whole[:, 0:128] + unpacked_rim(xr4[1, g].astype(F32), 0),
+                whole[:, 128:384],
+                whole[:, 384:512] + unpacked_rim(xr4[0, g].astype(F32), 96),
+            ],
+            axis=1,
         )
         for cc in range(2):
             part = whole[cc * 32 : cc * 32 + 32]
@@ -354,27 +406,28 @@
     couple_out,
 ):
     vmem = pl.BlockSpec(memory_space=pltpu.VMEM)
-    anyw = pl.BlockSpec(memory_space=pl.ANY)
+    hbm = pl.BlockSpec(memory_space=pltpu.HBM)
     n_copies = 64
     scratch = [
         pltpu.VMEM((NF, CK, EXT), BF),
         pltpu.VMEM((EXT, 1024), BF),
-        pltpu.VMEM((1024, ELEMS), BF),
+        pltpu.VMEM((2, 1024, HE), BF),
         pltpu.VMEM((168, 896), BF),
         pltpu.VMEM((168, 672), BF),
         pltpu.VMEM((224, 896), BF),
         pltpu.VMEM((224, 672), BF),
         pltpu.VMEM((168, 1024), BF),
-        pltpu.VMEM((168, EXT), BF),
+        pltpu.VMEM((168, PADK), BF),
         pltpu.VMEM((256, 1024), BF),
-        pltpu.VMEM((256, EXT), BF),
+        pltpu.VMEM((256, PADK), BF),
         pltpu.VMEM((168, ELEMS), F32),
-        pltpu.VMEM((NF, 192, ELEMS), BF),
-        pltpu.VMEM((NF, 192, ELEMS), BF),
+        pltpu.VMEM((2, NF, 192, HE), BF),
+        pltpu.VMEM((2, NF, 192, HE), BF),
         pltpu.VMEM((NF, CK, FACES), BF),
-        pltpu.VMEM((NF, CK, 128), BF),
-        pltpu.VMEM((NF, CK, 128), BF),
-        pltpu.VMEM((2, CK, 128), BF),
+        pltpu.VMEM((2, 16, 128), BF),
+        pltpu.VMEM((2, NF, 16, 128), BF),
+        pltpu.VMEM((2, 16, 128), BF),
+        pltpu.VMEM((2, NF, 16, 128), BF),
         pltpu.VMEM((CK, FACES), BF),
         pltpu.VMEM((CK, FACES), BF),
         pltpu.VMEM((CK, FACES), BF),
@@ -388,9 +441,17 @@
         pltpu.VMEM((2, 16, 128), F32),
         pltpu.VMEM((FACES, FACES), BF),
         pltpu.VMEM((CK, FACES), F32),
-        pltpu.VMEM((256, ELEMS), F32),
+        pltpu.VMEM((2, 256, HE), F32),
         pltpu.VMEM((CK, FACES), F32),
-        pltpu.SemaphoreType.DMA((4,)),
+        pltpu.VMEM((2, FACES), F32),
+        pltpu.VMEM((NFD, 2, FACES), F32),
+        pltpu.VMEM((4, ELEMS), I32),
+        pltpu.VMEM((1, ELEMS), I32),
+        pltpu.VMEM((NID, 2, ELEMS), BF),
+        pltpu.VMEM((1, FACES), I32),
+        pltpu.VMEM((1, ELEMS), F32),
+        pltpu.VMEM((2, 8), F32),
+        pltpu.SemaphoreType.DMA((12,)),
         pltpu.SemaphoreType.DMA((n_copies,)),
         pltpu.SemaphoreType.DMA((n_copies,)),
     ]
@@ -398,25 +459,25 @@
     new, mixed = pl.pallas_call(
         kernel,
         out_shape=(shape, shape),
-        in_specs=[vmem] * 8 + [anyw] * 4,
+        in_specs=[hbm] * 12,
         out_specs=(vmem, vmem),
         scratch_shapes=scratch,
         compiler_params=pltpu.CompilerParams(
-            collective_id=0, has_side_effects=True, vmem_limit_bytes=48 * 1024 * 1024
+            collective_id=0, has_side_effects=True, vmem_limit_bytes=62 * 1024 * 1024
         ),
     )(
+        line_diagonal,
         jnp.transpose(traces, (1, 0, 2)),
+        element_faces,
+        orders.reshape(1, ELEMS),
         jnp.transpose(interior_source, (1, 0, 2)),
-        orders.reshape(1, ELEMS),
+        couple_in,
+        trace_block,
+        local_inverse,
+        couple_out,
+        solver_slots.reshape(1, FACES),
         element_scale.reshape(1, ELEMS),
-        element_faces,
-        solver_slots.reshape(1, FACES),
-        line_diagonal,
         species_mix,
-        couple_in,
-        local_inverse,
-        trace_block,
-        couple_out,
     )
     return new, mixed
 

time: 58.7 us -> 48.6 us (0.83)
  local copies, waits for them, and re-layouts: 9.87 us -> 2.41 us
  Pallas kernels: 47.8 us -> 45.3 us
    unnamed x24 -> x2, local copies, waits for them, and re-layouts: 8.4 us -> 0.01 us
    pallas_call x1, Pallas kernels: 47.8 us -> 45.3 us  [shards(): pl.pallas_call(kernel, out_shape=(shape, shape), in_specs=[hbm] * 12, out...]
    pallas_call x2, local copies, waits for them, and re-layouts: 1.47 us -> 2.41 us  [shards(): pl.pallas_call(kernel, out_shape=(shape, shape), in_specs=[hbm] * 12, out...]
where the time goes in v2:
time: 48.6 us; the launch traced here: 48.4 us
  Pallas kernels  45.3 us (93%)
  local copies, waits for them, and re-layouts  2.41 us (5%)
  between operations  0.65 us (1%)
    pallas_call x1, Pallas kernels, shards(): pl.pallas_call(kernel, out_shape=(shape, shape), in_specs=[hbm] * 12, out...  45.3 us
    pallas_call x2, local copies, waits for them, and re-layouts, shards(): pl.pallas_call(kernel, out_shape=(shape, shape), in_specs=[hbm] * 12, out...  2.41 us

profile of v2, /device:TPU:1, one launch (start us, length us, event | category | flops | bytes accessed | tf_op | source)
XLA Modules:
  0.0 48.4 jit_solution(2090944895526927163)
XLA Ops:
  0.6 45.3 %shard_map.131 = (f32[2,28,512]{2,1,0:T(8,128)}, f32[2,28,512]{2,1,0:T(8,128)}) custom-call(f32[2,512]{1,0:T(2,128)} %dia_hbm.1, f32[28,2,512]{2,1,0:T(2,128)} %bitcast.5, s32[4,256]{1,0:T(4,128)} %fac_hbm.1, s32[1,256]{1,0:T(1,128)} %bitcast.8, bf16[84,2,256]{2,1,0:T(2,128)(2,1)} %bitcast.6, bf16[168,896]{1,0:T(8,128)(2,1)} %ci_hbm.1, ...), custom_call_target="tpu_custom_call" | custom-call | tf_op jit(solution)/shard_map/pallas_call | solution.py:459
  46.0 0.0 copy-start
  46.0 1.7 %copy.14 = f32[2,28,512]{2,0,1:T(2,128)} copy(f32[2,28,512]{2,1,0:T(8,128)} %get-tuple-element.2) | data formatting | bytes 229376 | tf_op jit(solution)/shard_map/pallas_call | solution.py:459
  47.7 0.0 copy-done
  47.7 0.7 %copy.15 = f32[2,28,512]{2,0,1:T(2,128)} copy(f32[2,28,512]{2,1,0:T(8,128)S(1)} %copy-done) | data formatting | bytes 229376 | tf_op jit(solution)/shard_map/pallas_call | solution.py:459
Async XLA Ops:
  46.0 1.7 %copy-start = (f32[2,28,512]{2,1,0:T(8,128)S(1)}, f32[2,28,512]{2,1,0:T(8,128)}, u32[]{:S(2)}) copy-start(f32[2,28,512]{2,1,0:T(8,128)} %get-tuple-element.3) | copy-start | bytes 344068

commit v3 on v2

--- a/solution.py
+++ b/solution.py
@@ -463,21 +463,21 @@
         out_specs=(vmem, vmem),
         scratch_shapes=scratch,
         compiler_params=pltpu.CompilerParams(
-            collective_id=0, has_side_effects=True, vmem_limit_bytes=62 * 1024 * 1024
+            collective_id=0, has_side_effects=True, vmem_limit_bytes=48 * 1024 * 1024
         ),
     )(
-        line_diagonal,
-        jnp.transpose(traces, (1, 0, 2)),
-        element_faces,
-        orders.reshape(1, ELEMS),
-        jnp.transpose(interior_source, (1, 0, 2)),
-        couple_in,
-        trace_block,
-        local_inverse,
-        couple_out,
-        solver_slots.reshape(1, FACES),
-        element_scale.reshape(1, ELEMS),
-        species_mix,
+        pltpu.with_memory_space_constraint(line_diagonal, pltpu.HBM),
+        pltpu.with_memory_space_constraint(jnp.transpose(traces, (1, 0, 2)), pltpu.HBM),
+        pltpu.with_memory_space_constraint(element_faces, pltpu.HBM),
+        pltpu.with_memory_space_constraint(orders.reshape(1, ELEMS), pltpu.HBM),
+        pltpu.with_memory_space_constraint(jnp.transpose(interior_source, (1, 0, 2)), pltpu.HBM),
+        pltpu.with_memory_space_constraint(couple_in, pltpu.HBM),
+        pltpu.with_memory_space_constraint(trace_block, pltpu.HBM),
+        pltpu.with_memory_space_constraint(local_inverse, pltpu.HBM),
+        pltpu.with_memory_space_constraint(couple_out, pltpu.HBM),
+        pltpu.with_memory_space_constraint(solver_slots.reshape(1, FACES), pltpu.HBM),
+        pltpu.with_memory_space_constraint(element_scale.reshape(1, ELEMS), pltpu.HBM),
+        pltpu.with_memory_space_constraint(species_mix, pltpu.HBM),
     )
     return new, mixed
 

time: 48.6 us -> 46.9 us (0.965)
  local copies, waits for them, and re-layouts: 2.41 us -> 1.47 us
  Pallas kernels: 45.3 us -> 44.6 us
    pallas_call x2, local copies, waits for them, and re-layouts: 2.41 us -> 1.47 us  [shards(): pl.pallas_call(kernel, out_shape=(shape, shape), in_specs=[hbm] * 12, out...]
    pallas_call x1, Pallas kernels: 45.3 us -> 44.6 us  [shards(): pl.pallas_call(kernel, out_shape=(shape, shape), in_specs=[hbm] * 12, out...]
where the time goes in v3:
time: 46.9 us; the launch traced here: 46.8 us
  Pallas kernels  44.6 us (95%)
  local copies, waits for them, and re-layouts  1.47 us (3%)
  between operations  0.64 us (1%)
    pallas_call x1, Pallas kernels, shards(): pl.pallas_call(kernel, out_shape=(shape, shape), in_specs=[hbm] * 12, out...  44.6 us
    pallas_call x2, local copies, waits for them, and re-layouts, shards(): pl.pallas_call(kernel, out_shape=(shape, shape), in_specs=[hbm] * 12, out...  1.47 us

profile of v3, /device:TPU:1, one launch (start us, length us, event | category | flops | bytes accessed | tf_op | source)
XLA Modules:
  0.0 46.8 jit_solution(8965277156390313457)
XLA Ops:
  0.6 44.6 %shard_map.131 = (f32[2,28,512]{2,1,0:T(8,128)S(1)}, f32[2,28,512]{2,1,0:T(8,128)S(1)}) custom-call(f32[2,512]{1,0:T(2,128)} %dia_hbm.1, f32[28,2,512]{2,1,0:T(2,128)} %bitcast.5, s32[4,256]{1,0:T(4,128)} %fac_hbm.1, s32[1,256]{1,0:T(1,128)} %bitcast.8, bf16[84,2,256]{2,1,0:T(2,128)(2,1)} %bitcast.6, bf16[168,896]{1,0:T(8,128)(2,1)} %ci_hbm.1, ...), custom_call_target="tpu_custom_call" | custom-call | tf_op jit(solution)/shard_map/pallas_call | solution.py:459
  45.3 0.7 %copy.14 = f32[2,28,512]{2,0,1:T(2,128)} copy(f32[2,28,512]{2,1,0:T(8,128)S(1)} %get-tuple-element.2) | data formatting | bytes 229376 | tf_op jit(solution)/shard_map/pallas_call | solution.py:459
  46.0 0.7 %copy.15 = f32[2,28,512]{2,0,1:T(2,128)} copy(f32[2,28,512]{2,1,0:T(8,128)S(1)} %get-tuple-element.3) | data formatting | bytes 229376 | tf_op jit(solution)/shard_map/pallas_call | solution.py:459

commit v4 on v3

--- a/solution.py
+++ b/solution.py
@@ -69,9 +69,9 @@
 def kernel(
     dia_hbm, tr_hbm, fac_hbm, ord_hbm, src_hbm, ci_hbm, tb_hbm, li_hbm, co_hbm, slot_hbm, scl_hbm, mix_hbm,
     new_ref, mixed_ref,
-    ta, oh, gat, civ, liv, tbv, cov, cip, lip, tbp, cop, srcf,
-    lo_all, in_all, ra, rim1, xr1, rim4, xr4, vb, ln, rn, ll, rr,
-    s1, r1, r2, r3, dt, dwin, pm, own32, tbg, ownres,
+    ta, oh, gat, civ, liv, tbv, cov, cip, lip, tbp, cop, cocol, srcf,
+    lo_all, mp, sb, rb, rim1, xr1, rim4, xr4, vb, ln, rn, ll, rr,
+    s1, r1, r2, r3, dt, dwin, pm, own32, tbg,
     dia_ref, tr_ref, fac_ref, ord_ref, src_ref, slot_ref, scl_ref, mix_ref,
     wsem, ssem, rsem,
 ):
@@ -88,9 +88,9 @@
         return (f + step) % NF
 
     pairs = (
-        (dia_hbm, dia_ref), (tr_hbm, tr_ref), (fac_hbm, fac_ref), (ord_hbm, ord_ref), (src_hbm, src_ref),
+        (tr_hbm, tr_ref), (dia_hbm, dia_ref), (fac_hbm, fac_ref), (ord_hbm, ord_ref), (src_hbm, src_ref),
         (ci_hbm, civ), (tb_hbm, tbv), (li_hbm, liv), (co_hbm, cov),
-        (slot_hbm, slot_ref), (scl_hbm, scl_ref), (mix_hbm, mix_ref),
+        (slot_hbm, slot_ref), (scl_hbm, scl_ref), (mix_hbm, mix_ref.at[f]),
     )
     fetch = [pltpu.make_async_copy(src, dst, wsem.at[i]) for i, (src, dst) in enumerate(pairs)]
     for c in fetch:
@@ -126,20 +126,14 @@
     for g in range(NF):
         for h in range(2):
             lo_all[h, g, 176:192, :] = pad16
-            in_all[h, g, 176:192, :] = pad16
 
     own32[...] = jnp.zeros((CK, FACES), F32)
-    fetch[1].wait()
+    fetch[0].wait()
     for c in range(2):
         own32[c * 32 : c * 32 + NFD, :] = tr_ref[:, c, :]
     ta[f, :, 0:FACES] = own32[...].astype(BF)
     rim1[0] = packed_rim(own32[:, 0:128], 0).astype(BF)
     rim1[1] = packed_rim(own32[:, 384:512], 96).astype(BF)
-    fetch[0].wait()
-    dia = jnp.concatenate([dia_ref[...]] * 4, axis=0)
-    for zz in range(8):
-        s1[zz] = pltpu.roll(dia, (8 - 64 * zz) % FACES, 1)[0:2, 0:128]
-
     pl.semaphore_wait(barrier, len(greet))
 
     ex1 = []
@@ -149,10 +143,33 @@
         ex1.append(send(rim1.at[0], xr1.at[1, f], dev))
     for dev in field_peers:
         ex1.append(send(ta.at[f, :, pl.ds(0, FACES)], ta.at[f, :, pl.ds(0, FACES)], dev))
+    fetch[11].wait()
+    exm = [send(mix_ref.at[f], mix_ref.at[f], dev) for dev in field_peers]
+    fetch[1].wait()
+    dia = jnp.concatenate([dia_ref[...]] * 4, axis=0)
+    for zz in range(8):
+        s1[zz] = pltpu.roll(dia, (8 - 64 * zz) % FACES, 1)[0:2, 0:128]
     dz = []
     for i in range(1, 8):
         dz.append(send(s1.at[(z + i) % 8], r1.at[z], z_peers[i - 1]))
     r1[z] = s1[z]
+
+    rown = iota((256, 224), 0)
+    rk = rown & 31
+    want_r = jnp.where(rk < NFD, ((rown >> 5) & 1) * 112 + (rown >> 6) * NFD + rk, -1)
+    permr = one_hot(iota((256, 224), 1) == want_r)
+    colw = iota((672, 1024), 1)
+    inn = colw & 255
+    permw = one_hot(iota((672, 1024), 0) == jnp.where(inn < 168, (colw >> 8) * 168 + inn, -1))
+    fetch[8].wait()
+    wide = dot(dot(permr, cov[...]).astype(BF), permw).astype(BF)
+    for g in range(NF):
+        cop[g] = wide[:, g * 256 : (g + 1) * 256]
+    half_rows = pl.ds(pl.multiple_of(k * 128, 128), 128)
+    exw = []
+    for i in range(1, NF):
+        exw.append(send(cop.at[field_at(i), half_rows], cocol.at[f, half_rows], field_peers[i - 1]))
+    cocol[f] = cop[f]
 
     fetch[2].wait()
     rel = (fac_ref[...] - d * FACES) & (ND * FACES - 1)
@@ -181,10 +198,6 @@
     permk = one_hot(iota((896, 1024), 0) == want)
     fetch[5].wait()
     cip[...] = dot(civ[...], permk).astype(BF)
-    rown = iota((256, 224), 0)
-    rk = rown & 31
-    want_r = jnp.where(rk < NFD, ((rown >> 5) & 1) * 112 + (rown >> 6) * NFD + rk, -1)
-    permr = one_hot(iota((256, 224), 1) == want_r)
     fetch[6].wait()
     tbp[...] = dot(dot(permr, tbv[...]).astype(BF), permk).astype(BF)
 
@@ -207,6 +220,12 @@
         lo_all[h, f, 0:176] = jnp.concatenate([loads, zero8], axis=0).astype(BF)
         for dev in field_peers:
             ex2[h].append(send(lo_all.at[h, f, pl.ds(0, 176)], lo_all.at[h, f, pl.ds(0, 176)], dev))
+    for c in exw:
+        c.wait_recv()
+    exf = []
+    for i in range(1, NF):
+        part = cocol.at[field_at(i), half_rows]
+        exf.append(send(part, part, core_peer))
     for c in dz:
         c.wait_recv()
     for c in range(2):
@@ -221,21 +240,53 @@
     perms = one_hot(iota((672, PADK), 0) == jnp.where(inn < 168, slab * 168 + inn, -1))
     fetch[7].wait()
     lip[...] = dot(liv[...], perms).astype(BF)
-    fetch[8].wait()
-    cop[...] = dot(dot(permr, cov[...]).astype(BF), perms).astype(BF)
     for h in range(2):
         tbg[h] = dot(tbp[...], gat[h])
 
-    ex3 = [[], []]
+    for c in exf:
+        c.wait_recv()
+    fetch[10].wait()
+    zero88 = jnp.zeros((88, HE), F32)
+    acc = None
     for h in range(2):
         es = slice(h * HE, h * HE + HE)
         for c in ex2[h]:
             c.wait_recv()
         inter = dot(lip[...], lo_all[h].reshape(PADK, HE))
         inter = jnp.where(inner_live[:, es], inter, 0.0)
-        in_all[h, f, 0:176] = jnp.concatenate([inter, zero8], axis=0).astype(BF)
-        for dev in field_peers:
-            ex3[h].append(send(in_all.at[h, f, pl.ds(0, 176)], in_all.at[h, f, pl.ds(0, 176)], dev))
+        inter = jnp.concatenate([inter, zero88], axis=0).astype(BF)
+        his, los = [], []
+        for g in range(NF):
+            blocks = dot(cocol[g], inter) + jnp.where(f == g, tbg[h], 0.0)
+            blocks = jnp.where(face_live[:, es], blocks, 0.0) * scl_ref[:, es]
+            flat = jnp.concatenate([blocks[j * CK : (j + 1) * CK] for j in range(4)], axis=1)
+            hi = flat.astype(BF)
+            his.append(hi)
+            los.append((flat - hi.astype(F32)).astype(BF))
+        part = dot_nt(jnp.concatenate(his + los, axis=0), oh[:, h * 512 : h * 512 + 512])
+        acc = part if acc is None else acc + part
+    res = acc[0:256] + acc[256:512]
+
+    for c in exm:
+        c.wait_recv()
+    for c in range(8):
+        share = res[c * 32 : c * 32 + 32]
+        for c2 in range(8):
+            share = share + mix_ref[c // 2, c % 2 : c % 2 + 1, c2 : c2 + 1] * res[c2 * 32 : c2 * 32 + 32]
+        mp[c // 2, (c % 2) * 32 : (c % 2) * 32 + 32, :] = share
+    for g in range(NF):
+        sb[g] = mp[g, :, 0:FACES].astype(BF)
+        rim = mp[g, :, FACES:EXT]
+        rim4[g, 0] = packed_rim(rim, 0).astype(BF)
+        rim4[g, 1] = packed_rim(rim, RIM).astype(BF)
+
+    ex4 = []
+    for i in range(NF):
+        ex4.append(send(rim4.at[field_at(i), 0], xr4.at[0, f], prev_all[i]))
+        ex4.append(send(rim4.at[field_at(i), 1], xr4.at[1, f], next_all[i]))
+    for i in range(1, NF):
+        ex4.append(send(sb.at[field_at(i)], rb.at[f], field_peers[i - 1]))
+
     for c in dy:
         c.wait_recv()
     dk = send(r2, r3.at[k], core_peer)
@@ -250,31 +301,6 @@
     slot_qt = moved[0:1] * 16 + moved[1:2]
     pm[...] = one_hot(iota((FACES, FACES), 0) == slot_qt)
 
-    fetch[10].wait()
-    fetch[11].wait()
-    acc = jnp.zeros((2 * CK, EXT), F32)
-    for h in range(2):
-        es = slice(h * HE, h * HE + HE)
-        for c in ex3[h]:
-            c.wait_recv()
-        blocks = tbg[h] + dot(cop[...], in_all[h].reshape(PADK, HE))
-        blocks = jnp.where(face_live[:, es], blocks, 0.0) * scl_ref[:, es]
-        wide = jnp.concatenate([blocks[j * CK : (j + 1) * CK] for j in range(4)], axis=1)
-        acc = acc + dot_nt(hi_lo(wide), oh[:, h * 512 : h * 512 + 512])
-    res = acc[0:CK] + acc[CK : 2 * CK]
-    ownres[...] = res[:, 0:FACES]
-    rim4[0] = packed_rim(res[:, FACES:EXT], 0).astype(BF)
-    rim4[1] = packed_rim(res[:, FACES:EXT], RIM).astype(BF)
-    ra[f] = res[:, 0:FACES].astype(BF)
-
-    ex4 = []
-    for dev in prev_all:
-        ex4.append(send(rim4.at[0], xr4.at[0, f], dev))
-    for dev in next_all:
-        ex4.append(send(rim4.at[1], xr4.at[1, f], dev))
-    for dev in field_peers:
-        ex4.append(send(ra.at[f], ra.at[f], dev))
-
     dk.wait_recv()
     r_i = iota((128, 128), 0)
     t_of = (r_i & 7) * 16 + ((r_i >> 3) & 7) * 2 + (r_i >> 6)
@@ -313,26 +339,19 @@
     for c in ex4:
         c.wait_recv()
 
-    mine = ownres[...]
-    mixed = [None, None]
-    for g in range(NF):
-        whole = jnp.where(f == g, mine, ra[g].astype(F32))
-        whole = jnp.concatenate(
-            [
-                whole[:, 0:128] + unpacked_rim(xr4[1, g].astype(F32), 0),
-                whole[:, 128:384],
-                whole[:, 384:512] + unpacked_rim(xr4[0, g].astype(F32), 96),
-            ],
-            axis=1,
-        )
-        for cc in range(2):
-            part = whole[cc * 32 : cc * 32 + 32]
-            for c in range(2):
-                coef = mix_ref[c : c + 1, 2 * g + cc : 2 * g + cc + 1]
-                coef = coef + jnp.where((f == g) & (c == cc), 1.0, 0.0)
-                term = coef * part
-                mixed[c] = term if mixed[c] is None else mixed[c] + term
-    both = jnp.concatenate(mixed, axis=0)
+    both = mp[f, :, 0:FACES]
+    for i in range(1, NF):
+        both = both + rb[field_at(i)].astype(F32)
+    to_last = sum(xr4[0, g].astype(F32) for g in range(NF))
+    to_first = sum(xr4[1, g].astype(F32) for g in range(NF))
+    both = jnp.concatenate(
+        [
+            both[:, 0:128] + unpacked_rim(to_first, 0),
+            both[:, 128:384],
+            both[:, 384:512] + unpacked_rim(to_last, 96),
+        ],
+        axis=1,
+    )
     moved_rhs = dot(hi_lo(both), pm[...])
     rhs = moved_rhs[0:CK] + moved_rhs[CK : 2 * CK]
     vb[...] = rhs.astype(BF)
@@ -344,7 +363,7 @@
         send(vb.at[:, pl.ds(0, 128)], rr, far[1]),
     ]
     for c in range(2):
-        mixed_ref[c] = mixed[c][0:NFD]
+        mixed_ref[c] = both[c * 32 : c * 32 + NFD]
     for c in ex5:
         c.wait_recv()
 
@@ -419,14 +438,16 @@
         pltpu.VMEM((168, 1024), BF),
         pltpu.VMEM((168, PADK), BF),
         pltpu.VMEM((256, 1024), BF),
-        pltpu.VMEM((256, PADK), BF),
+        pltpu.VMEM((NF, 256, 256), BF),
+        pltpu.VMEM((NF, 256, 256), BF),
         pltpu.VMEM((168, ELEMS), F32),
         pltpu.VMEM((2, NF, 192, HE), BF),
-        pltpu.VMEM((2, NF, 192, HE), BF),
+        pltpu.VMEM((NF, CK, EXT), F32),
+        pltpu.VMEM((NF, CK, FACES), BF),
         pltpu.VMEM((NF, CK, FACES), BF),
         pltpu.VMEM((2, 16, 128), BF),
         pltpu.VMEM((2, NF, 16, 128), BF),
-        pltpu.VMEM((2, 16, 128), BF),
+        pltpu.VMEM((NF, 2, 16, 128), BF),
         pltpu.VMEM((2, NF, 16, 128), BF),
         pltpu.VMEM((CK, FACES), BF),
         pltpu.VMEM((CK, FACES), BF),
@@ -442,7 +463,6 @@
         pltpu.VMEM((FACES, FACES), BF),
         pltpu.VMEM((CK, FACES), F32),
         pltpu.VMEM((2, 256, HE), F32),
-        pltpu.VMEM((CK, FACES), F32),
         pltpu.VMEM((2, FACES), F32),
         pltpu.VMEM((NFD, 2, FACES), F32),
         pltpu.VMEM((4, ELEMS), I32),
@@ -450,7 +470,7 @@
         pltpu.VMEM((NID, 2, ELEMS), BF),
         pltpu.VMEM((1, FACES), I32),
         pltpu.VMEM((1, ELEMS), F32),
-        pltpu.VMEM((2, 8), F32),
+        pltpu.VMEM((NF, 2, 8), F32),
         pltpu.SemaphoreType.DMA((12,)),
         pltpu.SemaphoreType.DMA((n_copies,)),
         pltpu.SemaphoreType.DMA((n_copies,)),

time: 46.9 us -> 44.3 us (0.945)
  Pallas kernels: 44.6 us -> 42.1 us
    pallas_call x1, Pallas kernels: 44.6 us -> 42.1 us  [shards(): pl.pallas_call(kernel, out_shape=(shape, shape), in_specs=[hbm] * 12, out...]
where the time goes in v4:
time: 44.3 us; the launch traced here: 44.2 us
  Pallas kernels  42.1 us (95%)
  local copies, waits for them, and re-layouts  1.47 us (3%)
  between operations  0.64 us (1%)
    pallas_call x1, Pallas kernels, shards(): pl.pallas_call(kernel, out_shape=(shape, shape), in_specs=[hbm] * 12, out...  42.1 us
    pallas_call x2, local copies, waits for them, and re-layouts, shards(): pl.pallas_call(kernel, out_shape=(shape, shape), in_specs=[hbm] * 12, out...  1.47 us

profile of v4, /device:TPU:1, one launch (start us, length us, event | category | flops | bytes accessed | tf_op | source)
XLA Modules:
  0.0 44.2 jit_solution(9134467239206023241)
XLA Ops:
  0.6 42.1 %shard_map.131 = (f32[2,28,512]{2,1,0:T(8,128)S(1)}, f32[2,28,512]{2,1,0:T(8,128)S(1)}) custom-call(f32[2,512]{1,0:T(2,128)} %dia_hbm.1, f32[28,2,512]{2,1,0:T(2,128)} %bitcast.5, s32[4,256]{1,0:T(4,128)} %fac_hbm.1, s32[1,256]{1,0:T(1,128)} %bitcast.8, bf16[84,2,256]{2,1,0:T(2,128)(2,1)} %bitcast.6, bf16[168,896]{1,0:T(8,128)(2,1)} %ci_hbm.1, ...), custom_call_target="tpu_custom_call" | custom-call | tf_op jit(solution)/shard_map/pallas_call | solution.py:479
  42.7 0.7 %copy.14 = f32[2,28,512]{2,0,1:T(2,128)} copy(f32[2,28,512]{2,1,0:T(8,128)S(1)} %get-tuple-element.2) | data formatting | bytes 229376 | tf_op jit(solution)/shard_map/pallas_call | solution.py:479
  43.5 0.7 %copy.15 = f32[2,28,512]{2,0,1:T(2,128)} copy(f32[2,28,512]{2,1,0:T(8,128)S(1)} %get-tuple-element.3) | data formatting | bytes 229376 | tf_op jit(solution)/shard_map/pallas_call | solution.py:479

commit v5 on v4

--- a/solution.py
+++ b/solution.py
@@ -71,7 +71,7 @@
     new_ref, mixed_ref,
     ta, oh, gat, civ, liv, tbv, cov, cip, lip, tbp, cop, cocol, srcf,
     lo_all, mp, sb, rb, rim1, xr1, rim4, xr4, vb, ln, rn, ll, rr,
-    s1, r1, r2, r3, dt, dwin, pm, own32, tbg,
+    s1, r1, r2, r3, dt, dwin, pm, own32, tbg, cf,
     dia_ref, tr_ref, fac_ref, ord_ref, src_ref, slot_ref, scl_ref, mix_ref,
     wsem, ssem, rsem,
 ):
@@ -220,6 +220,12 @@
         lo_all[h, f, 0:176] = jnp.concatenate([loads, zero8], axis=0).astype(BF)
         for dev in field_peers:
             ex2[h].append(send(lo_all.at[h, f, pl.ds(0, 176)], lo_all.at[h, f, pl.ds(0, 176)], dev))
+    for c in exm:
+        c.wait_recv()
+    for c in range(8):
+        for c2 in range(8):
+            coef = mix_ref[c // 2, c % 2 : c % 2 + 1, c2 : c2 + 1] + (1.0 if c == c2 else 0.0)
+            cf[c * 8 + c2] = jnp.broadcast_to(coef, (8, 128))
     for c in exw:
         c.wait_recv()
     exf = []
@@ -247,7 +253,16 @@
         c.wait_recv()
     fetch[10].wait()
     zero88 = jnp.zeros((88, HE), F32)
-    acc = None
+    def mixed_share(part, c):
+        total = None
+        for c2 in range(8):
+            coef = jnp.concatenate([cf[c * 8 + c2]] * 4, axis=0)
+            coef = jnp.concatenate([coef] * (part.shape[1] // 128), axis=1)
+            term = coef * part[c2 * 32 : c2 * 32 + 32]
+            total = term if total is None else total + term
+        return total
+
+    flats = []
     for h in range(2):
         es = slice(h * HE, h * HE + HE)
         for c in ex2[h]:
@@ -263,28 +278,29 @@
             hi = flat.astype(BF)
             his.append(hi)
             los.append((flat - hi.astype(F32)).astype(BF))
-        part = dot_nt(jnp.concatenate(his + los, axis=0), oh[:, h * 512 : h * 512 + 512])
-        acc = part if acc is None else acc + part
-    res = acc[0:256] + acc[256:512]
-
-    for c in exm:
-        c.wait_recv()
-    for c in range(8):
-        share = res[c * 32 : c * 32 + 32]
-        for c2 in range(8):
-            share = share + mix_ref[c // 2, c % 2 : c % 2 + 1, c2 : c2 + 1] * res[c2 * 32 : c2 * 32 + 32]
-        mp[c // 2, (c % 2) * 32 : (c % 2) * 32 + 32, :] = share
+        flats.append(jnp.concatenate(his + los, axis=0))
+        if h == 0:
+            rim_part = dot_nt(flats[0], oh[FACES:EXT, 0:512])
+            acc_part = dot_nt(flats[0], oh[0:FACES, 0:512])
+
+    rim_part = rim_part + dot_nt(flats[1], oh[FACES:EXT, 512:1024])
+    rim_part = rim_part[0:256] + rim_part[256:512]
     for g in range(NF):
-        sb[g] = mp[g, :, 0:FACES].astype(BF)
-        rim = mp[g, :, FACES:EXT]
+        rim = jnp.concatenate([mixed_share(rim_part, 2 * g), mixed_share(rim_part, 2 * g + 1)], axis=0)
         rim4[g, 0] = packed_rim(rim, 0).astype(BF)
         rim4[g, 1] = packed_rim(rim, RIM).astype(BF)
 
     ex4 = []
-    for i in range(NF):
+    for i in (2, 1, 3, 0):
         ex4.append(send(rim4.at[field_at(i), 0], xr4.at[0, f], prev_all[i]))
         ex4.append(send(rim4.at[field_at(i), 1], xr4.at[1, f], next_all[i]))
-    for i in range(1, NF):
+    acc_part = acc_part + dot_nt(flats[1], oh[0:FACES, 512:1024])
+    acc_part = acc_part[0:256] + acc_part[256:512]
+    for g in range(NF):
+        own = jnp.concatenate([mixed_share(acc_part, 2 * g), mixed_share(acc_part, 2 * g + 1)], axis=0)
+        mp[g] = own
+        sb[g] = own.astype(BF)
+    for i in (2, 1, 3):
         ex4.append(send(sb.at[field_at(i)], rb.at[f], field_peers[i - 1]))
 
     for c in dy:
@@ -339,7 +355,7 @@
     for c in ex4:
         c.wait_recv()
 
-    both = mp[f, :, 0:FACES]
+    both = mp[f]
     for i in range(1, NF):
         both = both + rb[field_at(i)].astype(F32)
     to_last = sum(xr4[0, g].astype(F32) for g in range(NF))
@@ -357,10 +373,10 @@
     vb[...] = rhs.astype(BF)
 
     ex5 = [
+        send(vb.at[:, pl.ds(384, 128)], ll, far[0]),
+        send(vb.at[:, pl.ds(0, 128)], rr, far[1]),
         send(vb, ln, (dom_at(1), f)),
         send(vb, rn, (dom_at(-1), f)),
-        send(vb.at[:, pl.ds(384, 128)], ll, far[0]),
-        send(vb.at[:, pl.ds(0, 128)], rr, far[1]),
     ]
     for c in range(2):
         mixed_ref[c] = both[c * 32 : c * 32 + NFD]
@@ -408,6 +424,12 @@
         new_ref[c] = new[c * 32 : c * 32 + NFD]
     for c in sent:
         c.wait_send()
+
+
+def turn(new_ref, mixed_ref, new_out, mixed_out):
+    for c in range(2):
+        new_out[:, c, :] = new_ref[c]
+        mixed_out[:, c, :] = mixed_ref[c]
 
 
 def shards(
@@ -442,7 +464,7 @@
         pltpu.VMEM((NF, 256, 256), BF),
         pltpu.VMEM((168, ELEMS), F32),
         pltpu.VMEM((2, NF, 192, HE), BF),
-        pltpu.VMEM((NF, CK, EXT), F32),
+        pltpu.VMEM((NF, CK, FACES), F32),
         pltpu.VMEM((NF, CK, FACES), BF),
         pltpu.VMEM((NF, CK, FACES), BF),
         pltpu.VMEM((2, 16, 128), BF),
@@ -463,6 +485,7 @@
         pltpu.VMEM((FACES, FACES), BF),
         pltpu.VMEM((CK, FACES), F32),
         pltpu.VMEM((2, 256, HE), F32),
+        pltpu.VMEM((64, 8, 128), F32),
         pltpu.VMEM((2, FACES), F32),
         pltpu.VMEM((NFD, 2, FACES), F32),
         pltpu.VMEM((4, ELEMS), I32),
@@ -499,7 +522,15 @@
         pltpu.with_memory_space_constraint(element_scale.reshape(1, ELEMS), pltpu.HBM),
         pltpu.with_memory_space_constraint(species_mix, pltpu.HBM),
     )
-    return new, mixed
+    turned = jax.ShapeDtypeStruct((NFD, 2, FACES), F32)
+    new, mixed = pl.pallas_call(
+        turn,
+        out_shape=(turned, turned),
+        in_specs=[vmem] * 2,
+        out_specs=(vmem, vmem),
+        compiler_params=pltpu.CompilerParams(vmem_limit_bytes=4 * 1024 * 1024),
+    )(new, mixed)
+    return jnp.transpose(new, (1, 0, 2)), jnp.transpose(mixed, (1, 0, 2))
 
 
 def solution(mesh):

time: 44.3 us -> 41.7 us (0.941)
  local copies, waits for them, and re-layouts: 1.47 us -> 0 us
  Pallas kernels: 42.1 us -> 40.7 us
    pallas_call x1, Pallas kernels: 42.1 us -> 39.9 us  [shards(): pl.pallas_call(kernel, out_shape=(shape, shape), in_specs=[hbm] * 12, out...]
    pallas_call x2 -> x0, local copies, waits for them, and re-layouts: 1.47 us -> none  [shards(): pl.pallas_call(kernel, out_shape=(shape, shape), in_specs=[hbm] * 12, out...]
    pallas_call x0 -> x1, Pallas kernels: none -> 0.72 us  [shards(): pl.pallas_call(turn, out_shape=(turned, turned), in_specs=[vmem] * 2, out...]
where the time goes in v5:
time: 41.7 us; the launch traced here: 41.3 us
  Pallas kernels  40.7 us (98%)
  between operations  0.64 us (2%)
    pallas_call x1, Pallas kernels, shards(): pl.pallas_call(kernel, out_shape=(shape, shape), in_specs=[hbm] * 12, out...  39.9 us

profile of v5, /device:TPU:1, one launch (start us, length us, event | category | flops | bytes accessed | tf_op | source)
XLA Modules:
  0.0 41.3 jit_solution(537113931283428682)
XLA Ops:
  0.6 39.9 %shard_map.131 = (f32[2,28,512]{2,1,0:T(8,128)S(1)}, f32[2,28,512]{2,1,0:T(8,128)S(1)}) custom-call(f32[2,512]{1,0:T(2,128)} %dia_hbm.1, f32[28,2,512]{2,1,0:T(2,128)} %bitcast.7, s32[4,256]{1,0:T(4,128)} %fac_hbm.1, s32[1,256]{1,0:T(1,128)} %bitcast.10, bf16[84,2,256]{2,1,0:T(2,128)(2,1)} %bitcast.8, bf16[168,896]{1,0:T(8,128)(2,1)} %ci_hbm.1, ...), custom_call_target="tpu_custom_call" | custom-call | tf_op jit(solution)/shard_map/pallas_call | solution.py:502
  40.6 0.7 %shard_map.132 = (f32[28,2,512]{2,1,0:T(2,128)}, f32[28,2,512]{2,1,0:T(2,128)}) custom-call(f32[2,28,512]{2,1,0:T(8,128)S(1)} %get-tuple-element.6.new_ref, f32[2,28,512]{2,1,0:T(8,128)S(1)} %get-tuple-element.7.mixed_ref), custom_call_target="tpu_custom_call" | custom-call | tf_op jit(solution)/shard_map/pallas_call | solution.py:526

commit v6 on v5

--- a/solution.py
+++ b/solution.py
@@ -97,6 +97,7 @@
         c.start()
 
     field_peers = [(d, field_at(i)) for i in range(1, NF)]
+    far_first = [field_peers[1], field_peers[0], field_peers[2]]
     next_all = [(dom_at(1), field_at(i)) for i in range(NF)]
     prev_all = [(dom_at(-1), field_at(i)) for i in range(NF)]
     far = [(dom_at(2), f), (dom_at(-2), f)]
@@ -141,7 +142,7 @@
         ex1.append(send(rim1.at[1], xr1.at[0, f], dev))
     for dev in prev_all:
         ex1.append(send(rim1.at[0], xr1.at[1, f], dev))
-    for dev in field_peers:
+    for dev in far_first:
         ex1.append(send(ta.at[f, :, pl.ds(0, FACES)], ta.at[f, :, pl.ds(0, FACES)], dev))
     fetch[11].wait()
     exm = [send(mix_ref.at[f], mix_ref.at[f], dev) for dev in field_peers]
@@ -198,15 +199,15 @@
     permk = one_hot(iota((896, 1024), 0) == want)
     fetch[5].wait()
     cip[...] = dot(civ[...], permk).astype(BF)
-    fetch[6].wait()
-    tbp[...] = dot(dot(permr, tbv[...]).astype(BF), permk).astype(BF)
-
-    for c in ex1:
+
+    for c in ex1[0:8]:
         c.wait_recv()
     for g in range(NF):
         ta[g, :, FACES:EXT] = (
             unpacked_rim(xr1[0, g].astype(F32), 0) + unpacked_rim(xr1[1, g].astype(F32), RIM)
         ).astype(BF)
+    for c in ex1[8:]:
+        c.wait_recv()
     tall = ta[...].reshape(256, EXT)
     ex2 = [[], []]
     for h in range(2):
@@ -218,7 +219,7 @@
         loads = srcf[:, es] - dot(cip[...], gat[h])
         loads = jnp.where(inner_live[:, es], loads, 0.0)
         lo_all[h, f, 0:176] = jnp.concatenate([loads, zero8], axis=0).astype(BF)
-        for dev in field_peers:
+        for dev in far_first:
             ex2[h].append(send(lo_all.at[h, f, pl.ds(0, 176)], lo_all.at[h, f, pl.ds(0, 176)], dev))
     for c in exm:
         c.wait_recv()
@@ -246,6 +247,8 @@
     perms = one_hot(iota((672, PADK), 0) == jnp.where(inn < 168, slab * 168 + inn, -1))
     fetch[7].wait()
     lip[...] = dot(liv[...], perms).astype(BF)
+    fetch[6].wait()
+    tbp[...] = dot(dot(permr, tbv[...]).astype(BF), permk).astype(BF)
     for h in range(2):
         tbg[h] = dot(tbp[...], gat[h])
 
@@ -378,6 +381,8 @@
         send(vb, ln, (dom_at(1), f)),
         send(vb, rn, (dom_at(-1), f)),
     ]
+    for c in sent[:-4]:
+        c.wait_send()
     for c in range(2):
         mixed_ref[c] = both[c * 32 : c * 32 + NFD]
     for c in ex5:
@@ -422,7 +427,7 @@
     new = own32[...] - (back[0:CK] + back[CK : 2 * CK])
     for c in range(2):
         new_ref[c] = new[c * 32 : c * 32 + NFD]
-    for c in sent:
+    for c in ex5:
         c.wait_send()
 
 

time: 41.7 us -> 41.8 us (level)
  the two profiles are of different devices: /device:TPU:1 before, /device:TPU:2 now
where the time goes in v6:
time: 41.8 us; the launch traced here: 41.7 us
  Pallas kernels  41.1 us (98%)
  between operations  0.64 us (2%)
    pallas_call x1, Pallas kernels, shards(): pl.pallas_call(kernel, out_shape=(shape, shape), in_specs=[hbm] * 12, out...  40.3 us

profile of v6, /device:TPU:2, one launch (start us, length us, event | category | flops | bytes accessed | tf_op | source)
XLA Modules:
  0.0 41.7 jit_solution(11215023957255852020)
XLA Ops:
  0.6 40.3 %shard_map.131 = (f32[2,28,512]{2,1,0:T(8,128)S(1)}, f32[2,28,512]{2,1,0:T(8,128)S(1)}) custom-call(f32[2,512]{1,0:T(2,128)} %dia_hbm.1, f32[28,2,512]{2,1,0:T(2,128)} %bitcast.7, s32[4,256]{1,0:T(4,128)} %fac_hbm.1, s32[1,256]{1,0:T(1,128)} %bitcast.10, bf16[84,2,256]{2,1,0:T(2,128)(2,1)} %bitcast.8, bf16[168,896]{1,0:T(8,128)(2,1)} %ci_hbm.1, ...), custom_call_target="tpu_custom_call" | custom-call | tf_op jit(solution)/shard_map/pallas_call | solution.py:507
  41.0 0.7 %shard_map.132 = (f32[28,2,512]{2,1,0:T(2,128)}, f32[28,2,512]{2,1,0:T(2,128)}) custom-call(f32[2,28,512]{2,1,0:T(8,128)S(1)} %get-tuple-element.6.new_ref, f32[2,28,512]{2,1,0:T(8,128)S(1)} %get-tuple-element.7.mixed_ref), custom_call_target="tpu_custom_call" | custom-call | tf_op jit(solution)/shard_map/pallas_call | solution.py:531

commit v7 on v6

--- a/solution.py
+++ b/solution.py
@@ -93,8 +93,7 @@
         (slot_hbm, slot_ref), (scl_hbm, scl_ref), (mix_hbm, mix_ref.at[f]),
     )
     fetch = [pltpu.make_async_copy(src, dst, wsem.at[i]) for i, (src, dst) in enumerate(pairs)]
-    for c in fetch:
-        c.start()
+    fetch[0].start()
 
     field_peers = [(d, field_at(i)) for i in range(1, NF)]
     far_first = [field_peers[1], field_peers[0], field_peers[2]]
@@ -104,10 +103,13 @@
     z_peers = [(((z + i) % 8) * 16 + d % 16, f) for i in range(1, 8)]
     y_peers = [(z * 16 + ((y + i) % 8) * 2 + k, f) for i in range(1, 8)]
     core_peer = (d + 1 - 2 * k, f)
-    greet = field_peers + next_all + prev_all + far + z_peers + y_peers
+    hops = [side[i] for i in (2, 1, 3, 0) for side in (next_all, prev_all)]
+    greet = hops + far_first + far + z_peers + y_peers
     barrier = pltpu.get_barrier_semaphore()
     for dev in greet:
         pl.semaphore_signal(barrier, inc=1, device_id=dev, device_id_type=MESH)
+    for c in fetch[1:]:
+        c.start()
 
     count = [0]
     sent = []

time: 41.8 us -> 41.8 us (level)
  no operation moved by 1% of the time
where the time goes in v7:
time: 41.8 us; the launch traced here: 41.6 us
  Pallas kernels  41 us (98%)
  between operations  0.64 us (2%)
    pallas_call x1, Pallas kernels, shards(): pl.pallas_call(kernel, out_shape=(shape, shape), in_specs=[hbm] * 12, out...  40.3 us

profile of v7, /device:TPU:2, one launch (start us, length us, event | category | flops | bytes accessed | tf_op | source)
XLA Modules:
  0.0 41.6 jit_solution(17718542962213087223)
XLA Ops:
  0.6 40.3 %shard_map.131 = (f32[2,28,512]{2,1,0:T(8,128)S(1)}, f32[2,28,512]{2,1,0:T(8,128)S(1)}) custom-call(f32[2,512]{1,0:T(2,128)} %dia_hbm.1, f32[28,2,512]{2,1,0:T(2,128)} %bitcast.7, s32[4,256]{1,0:T(4,128)} %fac_hbm.1, s32[1,256]{1,0:T(1,128)} %bitcast.10, bf16[84,2,256]{2,1,0:T(2,128)(2,1)} %bitcast.8, bf16[168,896]{1,0:T(8,128)(2,1)} %ci_hbm.1, ...), custom_call_target="tpu_custom_call" | custom-call | tf_op jit(solution)/shard_map/pallas_call | solution.py:509
  40.9 0.7 %shard_map.132 = (f32[28,2,512]{2,1,0:T(2,128)}, f32[28,2,512]{2,1,0:T(2,128)}) custom-call(f32[2,28,512]{2,1,0:T(8,128)S(1)} %get-tuple-element.6.new_ref, f32[2,28,512]{2,1,0:T(8,128)S(1)} %get-tuple-element.7.mixed_ref), custom_call_target="tpu_custom_call" | custom-call | tf_op jit(solution)/shard_map/pallas_call | solution.py:533

commit v8 on v7

--- a/solution.py
+++ b/solution.py
@@ -140,10 +140,9 @@
     pl.semaphore_wait(barrier, len(greet))
 
     ex1 = []
-    for dev in next_all:
-        ex1.append(send(rim1.at[1], xr1.at[0, f], dev))
-    for dev in prev_all:
-        ex1.append(send(rim1.at[0], xr1.at[1, f], dev))
+    for i in (2, 1, 3, 0):
+        ex1.append(send(rim1.at[1], xr1.at[0, f], next_all[i]))
+        ex1.append(send(rim1.at[0], xr1.at[1, f], prev_all[i]))
     for dev in far_first:
         ex1.append(send(ta.at[f, :, pl.ds(0, FACES)], ta.at[f, :, pl.ds(0, FACES)], dev))
     fetch[11].wait()

time: 41.8 us -> 41.5 us (level)
  no operation moved by 1% of the time
where the time goes in v8:
time: 41.5 us; the launch traced here: 41.4 us
  Pallas kernels  40.8 us (98%)
  between operations  0.64 us (2%)
    pallas_call x1, Pallas kernels, shards(): pl.pallas_call(kernel, out_shape=(shape, shape), in_specs=[hbm] * 12, out...  40 us

profile of v8, /device:TPU:2, one launch (start us, length us, event | category | flops | bytes accessed | tf_op | source)
XLA Modules:
  0.0 41.4 jit_solution(10232356654681969455)
XLA Ops:
  0.6 40.0 %shard_map.131 = (f32[2,28,512]{2,1,0:T(8,128)S(1)}, f32[2,28,512]{2,1,0:T(8,128)S(1)}) custom-call(f32[2,512]{1,0:T(2,128)} %dia_hbm.1, f32[28,2,512]{2,1,0:T(2,128)} %bitcast.7, s32[4,256]{1,0:T(4,128)} %fac_hbm.1, s32[1,256]{1,0:T(1,128)} %bitcast.10, bf16[84,2,256]{2,1,0:T(2,128)(2,1)} %bitcast.8, bf16[168,896]{1,0:T(8,128)(2,1)} %ci_hbm.1, ...), custom_call_target="tpu_custom_call" | custom-call | tf_op jit(solution)/shard_map/pallas_call | solution.py:508
  40.7 0.7 %shard_map.132 = (f32[28,2,512]{2,1,0:T(2,128)}, f32[28,2,512]{2,1,0:T(2,128)}) custom-call(f32[2,28,512]{2,1,0:T(8,128)S(1)} %get-tuple-element.6.new_ref, f32[2,28,512]{2,1,0:T(8,128)S(1)} %get-tuple-element.7.mixed_ref), custom_call_target="tpu_custom_call" | custom-call | tf_op jit(solution)/shard_map/pallas_call | solution.py:532
